TPU v7x, 32 devices: a whole 2x2x4 slice. The times are simulated.
32 devices in a mesh: row: 8 (over z, y), col: 4 (over x, core).
Axes of the slice: x: 2, y: 2, z: 4, core: 2. Of those that a mesh axis runs over, the one named last changes fastest.
Arguments:
- laplacian: float32 [23040, 23040], P('row', 'col'), may hold values from -1 to 1.12, as said below
- block: float32 [23040, 256], P(('row', 'col')), may hold values from -6 to 6
- bounds: float32 [2], replicated, may hold values from 0.25 to 2.1, as said below
Outputs:
- filtered: float32 [23040, 256], P(('row', 'col'))
- rayleigh: float32 [256, 256], replicated
Inputs may be any that keep to these rules, and one draw needn't show every extreme that they name: laplacian is symmetric; its diagonal entries lie in 0.88 to 1.12 and its other entries have magnitude at most 1.14 / sqrt(23040). bounds[0] lies in 0.25 to 0.40 and bounds[1] in 1.95 to 2.10.
All inputs are finite; a program needn't handle non-finite values.
Results may differ from a plain program's by a relative error of at most 0.00025.
Values sent between devices are 32-bit elements; how exact they have to be, the bound alone decides.
No kernel may reach another device: no remote copies, remote signals or barrier semaphores. Data moves between devices by JAX's collectives and lax.ppermute only.
A program may use at most 128 MiB of HBM per device.

v0:
```python
import jax
import jax.numpy as jnp
from jax import lax
from jax.sharding import PartitionSpec as P


def relayout(panel_rows, row_index, col_index, tile_rows, tile_cols):
    offset = col_index * tile_cols - row_index * tile_rows
    zeros_pad = jnp.zeros((tile_cols, panel_rows.shape[1]), jnp.float32)
    padded = jnp.concatenate([zeros_pad, panel_rows, zeros_pad], axis=0)
    start_row = jnp.clip(offset + tile_cols, 0, tile_rows + tile_cols)
    sliced = lax.dynamic_slice_in_dim(padded, start_row, tile_cols, 0)
    target = offset + lax.broadcasted_iota(jnp.int32, (tile_cols, 1), 0)
    inside = (target >= 0) & (target < tile_rows)
    return jnp.where(inside, sliced, 0.0)


def body(laplacian, block, bounds):
    row_index = lax.axis_index("row")
    col_index = lax.axis_index("col")
    tile_rows, tile_cols = laplacian.shape
    lower_bound = bounds[0]
    upper_bound = bounds[1]
    center = (upper_bound + lower_bound) * 0.5
    half_width = (upper_bound - lower_bound) * 0.5
    factor_two = 2.0 / half_width
    global_rows = row_index * tile_rows + lax.broadcasted_iota(jnp.int32, (tile_rows, tile_cols), 0)
    global_cols = col_index * tile_cols + lax.broadcasted_iota(jnp.int32, (tile_rows, tile_cols), 1)
    shifted = laplacian - center * (global_rows == global_cols).astype(jnp.float32)

    def through_columns(panel_rows):
        return lax.dot_general(
            shifted,
            panel_rows,
            (((0,), (0,)), ((), ())),
            precision=lax.Precision.HIGHEST,
            preferred_element_type=jnp.float32,
        )

    def through_rows(panel_cols):
        return jnp.dot(
            shifted, panel_cols, precision=lax.Precision.HIGHEST, preferred_element_type=jnp.float32
        )

    def gather_rows(values):
        return lax.all_gather(values, "col", axis=0, tiled=True)

    def gather_cols(values):
        return lax.all_gather(values, "row", axis=0, tiled=True)

    def column_sum(values):
        return lax.psum_scatter(values, "row", scatter_dimension=0, tiled=True)

    def row_sum(values):
        return lax.psum_scatter(values, "col", scatter_dimension=0, tiled=True)

    filter_one = column_sum(through_columns(gather_rows(block))) / half_width
    filter_two = factor_two * row_sum(through_rows(gather_cols(filter_one))) - block
    filter_three = factor_two * column_sum(through_columns(gather_rows(filter_two))) - filter_one
    filter_four = factor_two * row_sum(through_rows(gather_cols(filter_three))) - filter_two
    panel_four = gather_rows(filter_four)
    dims_inner = (((0,), (0,)), ((), ()))
    image_piece, moved_piece = (
        lax.psum_scatter(through_columns(panel_four), "row", scatter_dimension=0, tiled=True),
        lax.psum_scatter(
            relayout(panel_four, row_index, col_index, tile_rows, tile_cols),
            "row",
            scatter_dimension=0,
            tiled=True,
        ),
    )
    gram_part = lax.dot_general(
        moved_piece,
        moved_piece,
        dims_inner,
        precision=lax.Precision.HIGHEST,
        preferred_element_type=jnp.float32,
    )
    image_part = lax.dot_general(
        moved_piece,
        image_piece,
        dims_inner,
        precision=lax.Precision.HIGHEST,
        preferred_element_type=jnp.float32,
    )
    gram, projected = lax.psum((gram_part, image_part), ("row", "col"))
    projected = projected + center * gram
    projected = (projected + projected.T) * 0.5
    factor = jnp.linalg.cholesky(gram)
    first_solve = jax.scipy.linalg.solve_triangular(factor, projected, lower=True)
    rayleigh = jax.scipy.linalg.solve_triangular(factor, first_solve.T, lower=True)
    return (filter_four, rayleigh)


def solution(mesh):
    placed = (P("row", "col"), P(("row", "col"), None), P())
    return jax.shard_map(
        body, mesh=mesh, in_specs=placed, out_specs=(P(("row", "col"), None), P()), check_vma=False
    )
```

profile of v0, /device:TPU:1, one launch (start us, length us, event | category | flops | bytes accessed | tf_op | source)
XLA Modules:
  0.0 1403.4 jit_solution(2724271184021714918)
XLA Ops:
  10.6 28.9 %all-gather.6.cloned.1.call-done = f32[2880,256]{1,0:T(8,128)} async-done(((f32[720,256]{1,0:T(8,128)}), f32[2880,256]{1,0:T(8,128)}) %all-gather.6.cloned.1.call-update) | async-done | bytes 2949136 | tf_op jit(solution)/shard_map/all_gather | solution.py:46
  39.5 116.0 %fusion.22 = f32[5760,256]{1,0:T(8,128)} fusion(f32[2880,256]{1,0:T(8,128)} %all-gather.6.cloned.1.call-done, f32[2880,5760]{1,0:T(8,128)} %param.5, f32[]{:T(128)} %bitcast.1, s32[5760]{0:T(1024)S(1)} %iota_add_fusion.1, s32[2880]{0:T(1024)S(1)} %iota_add_fusion.2), kind=kOutput, calls=%fused_computation.58 | convolution fusion | flops 51010560000 | bytes 75237120 | tf_op jit(solution)/shard_map/dot_general | solution.py:32
  156.9 110.1 %reduce-scatter.7.cloned.1.call-done = f32[720,256]{1,0:T(8,128)} async-done(((f32[5760,256]{1,0:T(8,128)}), f32[720,256]{1,0:T(8,128)}) %reduce-scatter.7.cloned.1.call-update) | async-done | bytes 737296 | tf_op jit(solution)/shard_map/reduce_scatter | solution.py:52
  269.1 94.2 %all-gather.8.cloned.1.call-done = f32[5760,256]{1,0:T(8,128)} async-done(((f32[720,256]{1,0:T(8,128)}), f32[5760,256]{1,0:T(8,128)}) %all-gather.8.cloned.1.call-update) | async-done | bytes 5898256 | tf_op jit(solution)/shard_map/all_gather | solution.py:49
  363.3 72.5 %fusion.21 = f32[2880,256]{1,0:T(8,128)} fusion(f32[5760,256]{1,0:T(8,128)} %all-gather.8.cloned.1.call-done, f32[2880,5760]{1,0:T(8,128)} %param.5, f32[]{:T(128)} %bitcast.1, s32[5760]{0:T(1024)S(1)} %iota_add_fusion.1, s32[2880]{0:T(1024)S(1)} %iota_add_fusion.2), kind=kOutput, calls=%fused_computation.57 | convolution fusion | flops 51010560000 | bytes 75237120 | tf_op jit(solution)/shard_map/dot_general | solution.py:41
  436.0 35.6 %reduce-scatter.9.cloned.1.call-done = f32[720,256]{1,0:T(8,128)} async-done(((f32[2880,256]{1,0:T(8,128)}), f32[720,256]{1,0:T(8,128)}) %reduce-scatter.9.cloned.1.call-update) | async-done | bytes 737296 | tf_op jit(solution)/shard_map/reduce_scatter | solution.py:55
  473.8 27.9 %all-gather.10.cloned.1.call-done = f32[2880,256]{1,0:T(8,128)} async-done(((f32[720,256]{1,0:T(8,128)}), f32[2880,256]{1,0:T(8,128)}) %all-gather.10.cloned.1.call-update) | async-done | bytes 2949136 | tf_op jit(solution)/shard_map/all_gather | solution.py:46
  501.7 116.1 %fusion.20 = f32[5760,256]{1,0:T(8,128)} fusion(f32[2880,256]{1,0:T(8,128)} %all-gather.10.cloned.1.call-done, f32[2880,5760]{1,0:T(8,128)} %param.5, f32[]{:T(128)} %bitcast.1, s32[5760]{0:T(1024)S(1)} %iota_add_fusion.1, s32[2880]{0:T(1024)S(1)} %iota_add_fusion.2), kind=kOutput, calls=%fused_computation.56 | convolution fusion | flops 51010560000 | bytes 75237120 | tf_op jit(solution)/shard_map/dot_general | solution.py:32
  617.9 111.4 %reduce-scatter.11.cloned.1.call-done = f32[720,256]{1,0:T(8,128)} async-done(((f32[5760,256]{1,0:T(8,128)}), f32[720,256]{1,0:T(8,128)}) %reduce-scatter.11.cloned.1.call-update) | async-done | bytes 737296 | tf_op jit(solution)/shard_map/reduce_scatter | solution.py:52
  731.5 93.8 %all-gather.12.cloned.1.call-done = f32[5760,256]{1,0:T(8,128)} async-done(((f32[720,256]{1,0:T(8,128)}), f32[5760,256]{1,0:T(8,128)}) %all-gather.12.cloned.1.call-update) | async-done | bytes 5898256 | tf_op jit(solution)/shard_map/all_gather | solution.py:49
  825.4 72.5 %fusion.19 = f32[2880,256]{1,0:T(8,128)} fusion(f32[5760,256]{1,0:T(8,128)} %all-gather.12.cloned.1.call-done, f32[2880,5760]{1,0:T(8,128)} %param.5, f32[]{:T(128)} %bitcast.1, s32[5760]{0:T(1024)S(1)} %iota_add_fusion.1, s32[2880]{0:T(1024)S(1)} %iota_add_fusion.2), kind=kOutput, calls=%fused_computation.55 | convolution fusion | flops 51010560000 | bytes 75237120 | tf_op jit(solution)/shard_map/dot_general | solution.py:41
  898.0 35.7 %reduce-scatter.13.cloned.1.call-done = f32[720,256]{1,0:T(8,128)} async-done(((f32[2880,256]{1,0:T(8,128)}), f32[720,256]{1,0:T(8,128)}) %reduce-scatter.13.cloned.1.call-update) | async-done | bytes 737296 | tf_op jit(solution)/shard_map/reduce_scatter | solution.py:55
  935.8 27.9 %all-gather.14.cloned.1.call-done = f32[2880,256]{1,0:T(8,128)} async-done(((f32[720,256]{1,0:T(8,128)}), f32[2880,256]{1,0:T(8,128)}) %all-gather.14.cloned.1.call-update) | async-done | bytes 2949136 | tf_op jit(solution)/shard_map/all_gather | solution.py:46
  964.1 6.9 fusion.2
  971.1 115.5 %fusion.18 = f32[5760,256]{1,0:T(8,128)} fusion(f32[2880,256]{1,0:T(8,128)S(1)} %copy-done.3, f32[2880,5760]{1,0:T(8,128)} %param.5, f32[]{:T(128)} %bitcast.1, s32[5760]{0:T(1024)S(1)} %iota_add_fusion.1, s32[2880]{0:T(1024)S(1)} %iota_add_fusion.2), kind=kOutput, calls=%fused_computation.54 | convolution fusion | flops 51010560000 | bytes 75237120 | tf_op jit(solution)/shard_map/dot_general | solution.py:32
  1086.7 3.4 fusion.25
  1090.1 108.4 %reduce-scatter.17.cloned.1.call-done = f32[720,256]{1,0:T(8,128)} async-done(((f32[5760,256]{1,0:T(8,128)}), f32[720,256]{1,0:T(8,128)}) %reduce-scatter.17.cloned.1.call-update) | async-done | bytes 737296 | tf_op jit(solution)/shard_map/reduce_scatter | solution.py:64
  1198.6 3.4 fusion.26
  1202.0 129.7 %all-reduce.4.cloned.1.call-done = (f32[256,256]{0,1:T(8,128)}, f32[256,256]{0,1:T(8,128)}) async-done(((f32[256,256]{0,1:T(8,128)}, f32[256,256]{0,1:T(8,128)}), (f32[256,256]{0,1:T(8,128)}, f32[256,256]{0,1:T(8,128)})) %all-reduce.4.cloned.1.call-update) | async-done | bytes 524304 | tf_op jit(solution)/shard_map/psum | solution.py:86
  1334.1 11.7 cholesky.50
  1345.9 9.8 custom-call.14
  1356.2 11.9 cholesky.105
  1370.0 3.8 while.4
  1373.8 19.7 %custom-call.17 = f32[2,128,128]{1,2,0:T(8,128)S(1)} custom-call(f32[2,128,128]{2,1,0:T(8,128)S(1)} %get-tuple-element.18), custom_call_target="InvertDiagBlocksLowerTriangular" | custom-call | tf_op jit(solution)/shard_map/jit(_solve_triangular)/triangular_solve | solution.py:91
  (73 shorter events, 21.5 us)
Async XLA Ops:
  7.2 32.3 %all-gather.6.cloned.1.call-start = ((), (), s32[]{:S(2)}) async-start(), calls=%async_computation.6 | async-start | bytes 3686400 | tf_op jit(solution)/shard_map/all_gather | solution.py:46
  7.9 259.1 %reduce-scatter.7.cloned.1.call-start = ((), (), s32[]{:S(2)}) async-start(), calls=%async_computation.7 | async-start | bytes 6635520 | tf_op jit(solution)/shard_map/reduce_scatter | solution.py:52
  155.6 207.8 %all-gather.8.cloned.1.call-start = ((), (), s32[]{:S(2)}) async-start(), calls=%async_computation.8 | async-start | bytes 6635520 | tf_op jit(solution)/shard_map/all_gather | solution.py:49
  269.1 202.6 %copy-start.1 = (f32[720,256]{1,0:T(8,128)S(1)}, f32[720,256]{1,0:T(8,128)}, u32[]{:S(2)}) copy-start(f32[720,256]{1,0:T(8,128)} %param.6) | copy-start | bytes 2211844
  269.1 202.6 %reduce-scatter.9.cloned.1.call-start = ((), (), s32[]{:S(2)}) async-start(), calls=%async_computation.9 | async-start | bytes 3686400 | tf_op jit(solution)/shard_map/reduce_scatter | solution.py:55
  435.9 65.8 %all-gather.10.cloned.1.call-start = ((), (), s32[]{:S(2)}) async-start(), calls=%async_computation.10 | async-start | bytes 3686400 | tf_op jit(solution)/shard_map/all_gather | solution.py:46
  473.7 255.7 %copy-start.2 = (f32[720,256]{1,0:T(8,128)S(1)}, f32[720,256]{1,0:T(8,128)}, u32[]{:S(2)}) copy-start(f32[720,256]{1,0:T(8,128)} %reduce-scatter.7.cloned.1.call-done) | copy-start | bytes 2211844
  473.7 255.6 %reduce-scatter.11.cloned.1.call-start = ((), (), s32[]{:S(2)}) async-start(), calls=%async_computation.11 | async-start | bytes 6635520 | tf_op jit(solution)/shard_map/reduce_scatter | solution.py:52
  617.9 207.5 %all-gather.12.cloned.1.call-start = ((), (), s32[]{:S(2)}) async-start(), calls=%async_computation.12 | async-start | bytes 6635520 | tf_op jit(solution)/shard_map/all_gather | solution.py:49
  731.5 202.2 %copy-start = (f32[720,256]{1,0:T(8,128)S(1)}, f32[720,256]{1,0:T(8,128)}, u32[]{:S(2)}) copy-start(f32[720,256]{1,0:T(8,128)} %multiply_subtract_fusion.2) | copy-start | bytes 2211844
  731.5 202.2 %reduce-scatter.13.cloned.1.call-start = ((), (), s32[]{:S(2)}) async-start(), calls=%async_computation.13 | async-start | bytes 3686400 | tf_op jit(solution)/shard_map/reduce_scatter | solution.py:55
  897.9 65.8 %all-gather.14.cloned.1.call-start = ((), (), s32[]{:S(2)}) async-start(), calls=%async_computation.14 | async-start | bytes 3686400 | tf_op jit(solution)/shard_map/all_gather | solution.py:46
  935.8 150.9 %reduce-scatter.15.cloned.1.call-start = ((), (), s32[]{:S(2)}) async-start(), calls=%async_computation.15 | async-start | bytes 6635520 | tf_op jit(solution)/shard_map/reduce_scatter | solution.py:65
  963.7 7.3 copy-start.3
  971.0 227.5 %reduce-scatter.17.cloned.1.call-start = ((), (), s32[]{:S(2)}) async-start(), calls=%async_computation.16 | async-start | bytes 6635520 | tf_op jit(solution)/shard_map/reduce_scatter | solution.py:64
  1086.6 245.1 %all-reduce.4.cloned.1.call-start = ((), (), s32[]{:S(2)}) async-start(), calls=%async_computation.17 | async-start | bytes 1048576 | tf_op jit(solution)/shard_map/psum | solution.py:86
Sparse Core Ops, SparseCore 0:
  9.6 29.8 all-gather.5
  155.7 111.2 reduce-scatter.6
  269.8 93.5 all-gather.7
  436.0 35.5 reduce-scatter.8
  473.8 27.8 all-gather.9
  618.0 111.3 reduce-scatter.10
  731.8 93.5 all-gather.11
  898.0 35.5 reduce-scatter.12
  935.9 27.8 all-gather.13
  971.1 111.8 reduce-scatter.14
  1086.7 111.7 reduce-scatter.16
  1204.4 127.2 all-reduce.3
where the time goes:
time: 1420 us; the launch traced here: 1400 us
  waiting for transfers between devices  805 us (57%)
  matrix products  502 us (35%)
  other arithmetic  70.8 us (5%)
  between operations  18.5 us (1%)
    dot_general x3, matrix products, through_columns(): lax.dot_general(shifted, panel_rows, (((0,), (0,)), ((), ())), precision=...  348 us
    reduce_scatter x2, waiting for transfers between devices, column_sum(): return lax.psum_scatter(values, 'row', scatter_dimension=0, tiled=True)  222 us
    all_gather x2, waiting for transfers between devices, gather_cols(): return lax.all_gather(values, 'row', axis=0, tiled=True)  188 us
    dot_general x2, matrix products, through_rows(): jnp.dot(shifted, panel_cols, precision=lax.Precision.HIGHEST, preferred_e...  145 us
    psum x1, waiting for transfers between devices, body(): gram, projected = lax.psum((gram_part, image_part), ('row', 'col'))  130 us
    reduce_scatter x1, waiting for transfers between devices, body(): lax.psum_scatter(through_columns(panel_four), 'row', scatter_dimension=0,...  108 us
    all_gather x3, waiting for transfers between devices, gather_rows(): return lax.all_gather(values, 'col', axis=0, tiled=True)  84.7 us
    reduce_scatter x2, waiting for transfers between devices, row_sum(): return lax.psum_scatter(values, 'col', scatter_dimension=0, tiled=True)  71.3 us
  transfers between devices with their start and end apart: 12, of which 11 were waited for; matrix products, arithmetic and copies ran while one was open for 9% of the time, Pallas kernels for 0%

commit v1 on v0

v1 whole, which is shorter than its diff:
```python
import functools

import jax
import jax.numpy as jnp
from jax import lax
from jax.experimental import pallas as pl
from jax.experimental.pallas import tpu as pltpu
from jax.sharding import PartitionSpec as P

F32 = jnp.float32
BF16 = jnp.bfloat16
LANES = 128
NT = (((1,), (1,)), ((), ()))
NN = (((1,), (0,)), ((), ()))
BOTH = ("row", "col")
RING = (0, 2, 4, 6, 7, 5, 3, 1)
RING_AT = tuple(RING.index(r) for r in range(8))

dot32 = functools.partial(lax.dot_general, preferred_element_type=F32)
dot_exact = functools.partial(
    lax.dot_general, precision=lax.Precision.HIGHEST, preferred_element_type=F32
)


def split(values):
    high = values.astype(BF16)
    return high, (values - high.astype(F32)).astype(BF16)


def pick(table, index):
    return jnp.asarray(table, jnp.int32)[index]


def after(value, *others):
    return lax.optimization_barrier((value, others))[0]


SLOTS = 3


def stream(source_ref, slots, sems, steps, corner, use):
    _, height, width = slots.shape

    def copy(step):
        row0, col0 = corner(step)
        slot = lax.rem(step, SLOTS)
        rows = pl.ds(pl.multiple_of(row0, 8), height)
        cols = pl.ds(pl.multiple_of(col0, LANES), width)
        return pltpu.make_async_copy(source_ref.at[rows, cols], slots.at[slot], sems.at[slot])

    for step in range(min(SLOTS - 1, steps)):
        copy(jnp.int32(step)).start()

    def one(step, carry):
        copy(step).wait()

        @pl.when(step + SLOTS - 1 < steps)
        def _():
            copy(step + SLOTS - 1).start()

        use(step, lax.rem(step, SLOTS))
        return carry

    lax.fori_loop(0, steps, one, 0)


def unit_start(place, aways, index, blocks):
    away = jnp.int32(aways[0])
    for i, a in enumerate(aways[1:], 1):
        away = jnp.where(index == i, a, away)
    return lax.rem(place + away + 8, 8) * blocks // 8 * LANES


def minus_center(block, center, delta):
    rows = lax.broadcasted_iota(jnp.int32, block.shape, 0)
    cols = lax.broadcasted_iota(jnp.int32, block.shape, 1)
    return block - jnp.where(rows - cols == delta, center, 0.0)


def with_center(slots, slot, center, row0, col0, offset, use):
    _, height, width = slots.shape
    hit = (offset >= 0) & (row0 + offset < col0 + width) & (row0 + offset + height > col0)

    @pl.when(hit)
    def _():
        use(minus_center(slots[slot], center, col0 - row0 - offset))

    @pl.when(jnp.logical_not(hit))
    def _():
        use(slots[slot])


VMEM = pl.BlockSpec(memory_space=pltpu.VMEM)
SMEM = pl.BlockSpec(memory_space=pltpu.SMEM)
ANY = pl.BlockSpec(memory_space=pl.ANY)


def kernel_params(count, chunks, depth, width, vectors):
    return dict(
        compiler_params=pltpu.CompilerParams(vmem_limit_bytes=56 * 2**20),
        cost_estimate=pl.CostEstimate(
            flops=6 * count * chunks * depth * width * vectors,
            bytes_accessed=4 * count * chunks * depth * width,
            transcendentals=0,
        ),
    )


def columns_product(laplacian, scalars, center, panel, aways, depth, width, first_chunk=0, totals=None):
    count, chunks = len(aways), len(panel)
    heights = [p.shape[0] for p in panel[0]]
    vectors, per = sum(heights), len(heights)
    blocks = laplacian.shape[1] // LANES

    def kernel(scalars_ref, center_ref, tile_ref, *refs):
        pieces = refs[: per * chunks]
        total_ref = None if totals is None else refs[per * chunks]
        out_ref, slots, high_ref, low_ref, sems = refs[-5:]

        def corner(step):
            chunk = lax.bitwise_xor(first_chunk + lax.rem(step, chunks), scalars_ref[2])
            return chunk * depth, unit_start(scalars_ref[0], aways, step // chunks, blocks)

        def use(step, slot):
            chunk, unit = lax.rem(step, chunks), step // chunks

            @pl.when(step == 0)
            def _():
                for c in range(chunks):
                    at = 0
                    for q in range(per):
                        high, low = split(pieces[c * per + q][:, :depth])
                        high_ref[c, at : at + heights[q]] = high
                        low_ref[c, at : at + heights[q]] = low
                        at += heights[q]

            def add(block):
                high, low = split(block)
                z_high, z_low = high_ref[chunk], low_ref[chunk]
                term = dot32(z_high, high, NN) + dot32(z_low, high, NN) + dot32(z_high, low, NN)

                @pl.when(chunk == 0)
                def _():
                    if total_ref is None:
                        out_ref[unit] = term
                    else:
                        out_ref[unit] = total_ref[unit] + term

                @pl.when(chunk > 0)
                def _():
                    out_ref[unit] += term

            row0, col0 = corner(step)
            with_center(slots, slot, center_ref[0], row0, col0, scalars_ref[1], add)

        stream(tile_ref, slots, sems, count * chunks, corner, use)

    given = [] if totals is None else [totals]
    return pl.pallas_call(
        kernel,
        out_shape=jax.ShapeDtypeStruct((count, vectors, width), F32),
        in_specs=[SMEM, SMEM, ANY] + [VMEM] * (per * chunks + len(given)),
        out_specs=VMEM,
        scratch_shapes=[
            pltpu.VMEM((SLOTS, depth, width), F32),
            pltpu.VMEM((chunks, vectors, depth), BF16),
            pltpu.VMEM((chunks, vectors, depth), BF16),
            pltpu.SemaphoreType.DMA((SLOTS,)),
        ],
        name="columns_product",
        **kernel_params(count, chunks, depth, width, vectors),
    )(scalars, center, laplacian, *[p for pieces in panel for p in pieces], *given)


def rows_product(laplacian, scalars, center, units, aways, totals, chunks, depth, lanes):
    count, number = len(units), len(chunks)
    width = units[0][0].shape[1]
    vectors = sum(p.shape[0] for p in units[0])
    flat = [p for pieces in units for p in pieces]
    blocks = laplacian.shape[1] // LANES

    def kernel(scalars_ref, center_ref, tile_ref, *refs):
        pieces = list(refs[: len(flat)])
        total_ref = None if totals is None else refs[len(flat)]
        out_ref, slots, high_ref, low_ref, sems = refs[-5:]

        def corner(step):
            first = (chunks[0] + step // count) * depth
            return first, unit_start(scalars_ref[0], aways, lax.rem(step, count), blocks)

        def use(step, slot):
            chunk, unit = step // count, lax.rem(step, count)

            @pl.when(step == 0)
            def _():
                rest = list(pieces)
                for u in range(count):
                    at = 0
                    for _ in units[u]:
                        piece = rest.pop(0)
                        high, low = split(piece[...])
                        high_ref[u, at : at + piece.shape[0]] = high
                        low_ref[u, at : at + piece.shape[0]] = low
                        at += piece.shape[0]
                if lanes > depth:
                    out_ref[:, :, depth:] = jnp.zeros((number, vectors, lanes - depth), F32)

            def add(block):
                high, low = split(block)
                z_high, z_low = high_ref[unit], low_ref[unit]
                term = dot32(z_high, high, NT) + dot32(z_low, high, NT) + dot32(z_high, low, NT)

                @pl.when(unit == 0)
                def _():
                    if total_ref is None:
                        out_ref[chunk, :, :depth] = term
                    else:
                        out_ref[chunk, :, :depth] = total_ref[chunk, :, :depth] + term

                @pl.when(unit > 0)
                def _():
                    out_ref[chunk, :, :depth] += term

            row0, col0 = corner(step)
            with_center(slots, slot, center_ref[0], row0, col0, scalars_ref[1], add)

        stream(tile_ref, slots, sems, count * number, corner, use)

    given = [] if totals is None else [totals]
    specs = []
    if given:
        first, shape = chunks[0], (number, vectors, lanes)
        whole = totals.shape[0] == number
        specs = [VMEM if whole else pl.BlockSpec(shape, lambda _: (first, 0, 0))]
    return pl.pallas_call(
        kernel,
        grid=(1,),
        out_shape=jax.ShapeDtypeStruct((number, vectors, lanes), F32),
        in_specs=[SMEM, SMEM, ANY] + [VMEM] * len(flat) + specs,
        out_specs=VMEM,
        scratch_shapes=[
            pltpu.VMEM((SLOTS, depth, width), F32),
            pltpu.VMEM((count, vectors, width), BF16),
            pltpu.VMEM((count, vectors, width), BF16),
            pltpu.SemaphoreType.DMA((SLOTS,)),
        ],
        name="rows_product",
        **kernel_params(count, number, depth, width, vectors),
    )(scalars, center, laplacian, *flat, *given)


def inverse_factor(gram):
    size = gram.shape[0]
    tall = 32

    def kernel(gram_ref, out_ref, work):
        work[...] = gram_ref[...]
        lane = lax.broadcasted_iota(jnp.int32, (1, size), 1)
        below = lax.broadcasted_iota(jnp.int32, (tall, 1), 0)
        for first in range(0, size, tall):
            rows = work[first : first + tall]
            for q in range(0, tall, 2):
                k = first + q
                col1 = jnp.broadcast_to(rows[:, k : k + 1], rows.shape)
                col2 = jnp.broadcast_to(rows[:, k + 1 : k + 2], rows.shape)
                over1 = lax.rsqrt(col1[q : q + 1])
                cross = col2[q : q + 1] * over1
                over2 = lax.rsqrt(col2[q + 1 : q + 2] - cross * cross)
                row1 = jnp.where(lane == k, 1.0, jnp.where(lane == k + 1, 0.0, rows[q : q + 1])) * over1
                row2 = jnp.where(lane == k + 1, 1.0, jnp.where(lane == k, 0.0, rows[q + 1 : q + 2]))
                row2 = (row2 - cross * row1) * over2
                times1 = col1 * over1
                times2 = (col2 - times1 * cross) * over2
                kept = jnp.where((lane == k) | (lane == k + 1), 0.0, rows)
                rows = jnp.where(
                    below > q + 1,
                    kept - times1 * row1 - times2 * row2,
                    jnp.where(below == q, row1, jnp.where(below == q + 1, row2, rows)),
                )
            rows = jnp.where((lane > first + below) & (lane < first + tall), 0.0, rows)
            work[first : first + tall] = rows
            rest = first + tall
            if rest < size:
                update = dot_exact(rows, rows, (((0,), (0,)), ((), ())))
                done = (lane >= first) & (lane < rest)
                work[rest:] = jnp.where(done, 0.0, work[rest:]) - update[rest:]
        at_row = lax.broadcasted_iota(jnp.int32, (size, size), 0)
        at_lane = lax.broadcasted_iota(jnp.int32, (size, size), 1)
        out_ref[...] = jnp.where(at_lane <= at_row, work[...], 0.0)

    return pl.pallas_call(
        kernel,
        out_shape=jax.ShapeDtypeStruct((size, size), F32),
        in_specs=[VMEM],
        out_specs=VMEM,
        scratch_shapes=[pltpu.VMEM((size, size), F32)],
        cost_estimate=pl.CostEstimate(flops=2 * size**3, bytes_accessed=8 * size**2, transcendentals=2 * size),
        name="inverse_factor",
    )(gram)


def swap(values, axis, mask):
    size = lax.axis_size(axis)
    return lax.ppermute(values, axis, [(i, i ^ mask) for i in range(size)])


def around(values, way):
    return lax.ppermute(values, "row", [(RING[p], RING[(p + way) % 8]) for p in range(8)])


def sum_stages(partial):
    row, col = lax.axis_index("row"), lax.axis_index("col")
    stages = (("col", 1, col & 1), ("col", 2, (col >> 1) & 1), ("row", 1, row & 1))
    values = partial
    for axis, mask, bit in stages:
        half = values.shape[0] // 2
        low, high = values[:half], values[half:]
        keep = jnp.where(bit == 0, low, high)
        send = jnp.where(bit == 0, high, low)
        values = keep + swap(send, axis, mask)
        yield values
    terms = [values] + [swap(values, "row", mask) for mask in (2, 4, 6)]
    z = row >> 1
    ordered = []
    for place in range(4):
        which = z ^ place
        ordered.append(jnp.where(which == 0, terms[0], jnp.where(which == 1, terms[1], jnp.where(which == 2, terms[2], terms[3]))))
    values = (ordered[0] + ordered[1]) + (ordered[2] + ordered[3])
    yield values
    for axis, mask, bit in reversed(stages):
        other = swap(values, axis, mask)
        low = jnp.where(bit == 0, values, other)
        high = jnp.where(bit == 0, other, values)
        values = jnp.concatenate([low, high], axis=0)
        yield values


def tuned_body(laplacian, block, bounds):
    tile_rows, tile_cols = laplacian.shape
    own_rows, vectors = block.shape
    half = vectors // 2
    depth = tile_rows // 2
    lanes = -(-depth // LANES) * LANES
    row, col = lax.axis_index("row"), lax.axis_index("col")
    core, x_at = col & 1, col >> 1
    place = pick(RING_AT, row)
    blocks = tile_cols // LANES
    starts = tuple(blocks * p // 8 for p in range(9))
    width = LANES * max(b - a for a, b in zip(starts, starts[1:]))
    center = (bounds[1] + bounds[0]) * 0.5
    half_width = (bounds[1] - bounds[0]) * 0.5
    factor_two = 2.0 / half_width
    centers = center.reshape(1)
    valid = lax.broadcasted_iota(jnp.int32, (1, width), 1) < (pick(starts, place + 1) - pick(starts, place)) * LANES
    per_tile = tile_cols // tile_rows
    offset = jnp.where(row // per_tile == col, (row % per_tile) * tile_rows, -1)
    scalars, turned_scalars = (jnp.stack([place, offset, f]).astype(jnp.int32) for f in (jnp.int32(0), x_at))

    def through_columns(here, rest, scalars=scalars, before=None):
        def product(call, aways, panel, **more):
            told = scalars if before is None else after(scalars, *before(call))
            return columns_product(laplacian, told, centers, panel, aways, depth, width, **more)

        begun_far = product(0, (4,), [here])
        begun = product(0, (3, -3), [here])
        there = rest(begun_far, begun)
        panel = [here, there]
        far = product(1, (4,), [there], first_chunk=1, totals=begun_far)[0]
        right, left = around(far[:half], 1), around(far[half:], -1)
        ahead, behind = product(2, (3, -3), [there], first_chunk=1, totals=begun)
        ahead = jnp.concatenate([ahead[:half] + right, ahead[half:]], 0)
        behind = jnp.concatenate([behind[:half], behind[half:] + left], 0)
        right, left = around(ahead, 1), around(behind, -1)
        ahead, behind = product(3, (2, -2), panel)
        right, left = around(ahead + right, 1), around(behind + left, -1)
        ahead, behind, own = product(4, (1, -1, 0), panel)
        ahead, behind = ahead + right, behind + left
        return panel, (own, around(ahead, 1), around(behind, -1)), ahead

    def through_rows(unit, before):
        unit = jnp.where(valid, unit, 0.0)

        def product(aways, units, totals, chunks):
            return rows_product(laplacian, scalars, centers, units, aways, totals, chunks, depth, lanes)

        right, left = around(unit, 1), around(unit, -1)
        totals = product((0,), [[unit]], None, (0, 1))
        right, left = after(right, totals), after(left, totals)
        right2, left2 = around(right, 1), around(left, -1)
        totals = product((-1, 1), [[right], [left]], totals, (0, 1))
        right2, left2 = after(right2, totals), after(left2, totals)
        right3, left3 = around(right2, 1), around(left2, -1)
        totals = product((-2, 2), [[right2], [left2]], totals, (0, 1))
        right3, left3 = after(right3, totals), after(left3, totals)
        far = [around(right3[:half], 1), around(left3[half:], -1)]
        first = product((-3, 3), [[right3], [left3]], totals, (0,))
        first = product((4,), [far], first, (0,))[0]
        first = first[:half] + swap(first[half:], "col", 1)
        second = product((-3, 3, 4), [[right3], [left3], far], after(totals, first), (1,))[0]
        first = factor_two * (first + swap(first, "col", 2)) - before[0][0]
        second = after(second[:half] + swap(second[half:], "col", 1), first)
        second_there = swap(second, "col", 2)

        def rest(*others):
            new = after(factor_two * (second + second_there) - before[1][0], *others)
            return new, swap(new, "col", 1)

        return (first, swap(first, "col", 1)), rest

    away_block = swap(block, "col", 2)
    chip = [block, swap(block, "col", 1)]
    away_chip = [away_block, swap(away_block, "col", 1)]

    def turned(pair):
        mine, other = pair[0].T, pair[1].T
        both = jnp.where(core == 0, jnp.concatenate([mine, other], 1), jnp.concatenate([other, mine], 1))
        both = jnp.pad(both, ((0, 0), (0, lanes - depth)))
        return jnp.where(core == 0, both[:half], both[half:]), jnp.where(core == 0, both[half:], both[:half])

    here, there = turned(chip), turned(away_chip)
    panel = [(jnp.where(x_at == 0, here[0], there[0]),), (jnp.where(x_at == 0, there[0], here[0]),)]

    _, terms, _ = through_columns(here, lambda *_: there, turned_scalars)
    filter_one = sum(terms) / half_width
    panel_two, terms, _ = through_columns(*through_rows(filter_one, panel))
    filter_three = factor_two * sum(terms) - filter_one

    def straight(pieces):
        mine, other = pieces
        return jnp.where(core == 0, jnp.concatenate([mine, other], 0), jnp.concatenate([other, mine], 0))

    held = []

    def whole_panel(here, there):
        chunks = [straight(pair)[:, :depth] for pair in (here, there)]
        chunk = jnp.where(x_at == 0, chunks[0], chunks[1])
        own = jnp.where(core == 0, chunk[:, :own_rows], chunk[:, own_rows:])
        held.append(sum_stages(dot_exact(own, own, NT)))
        return chunks, own

    def before(call):
        for _ in range((0, 0, 1, 3, 3)[call]):
            held.append(next(held[0]))
        return held[-1:] if call > 1 else []

    here, rest = through_rows(filter_three, panel_two)
    got = []

    def rest_and_gram(*others):
        there = rest(*others)
        got.append(whole_panel(here, there))
        return there

    _, (image, from_left, from_right), last_sent = through_columns(here, rest_and_gram, before=before)
    panel_chunks, own = got[0]
    filtered = own.T

    lead = LANES
    padded = jnp.concatenate([jnp.zeros((vectors, lead), F32)] + panel_chunks, 1)
    part = row % per_tile
    send_from = pick(starts, 4 * part + col) * LANES - part * tile_rows + lead
    sent = lax.dynamic_slice_in_dim(padded, send_from, width, 1)
    pairs = [
        (4 * r + c, 4 * RING[4 * (r % per_tile) + c] + r // per_tile) for r in range(8) for c in range(4)
    ]
    moved = lax.ppermute(sent, BOTH, pairs)
    over = tile_rows - starts[4] * LANES
    head = lax.ppermute(
        panel_chunks[1][:, depth - over :], BOTH, [(4 * (per_tile * c), 4 * RING[4] + c) for c in range(4)]
    )
    moved = jnp.where(valid, moved + jnp.pad(head, ((0, 0), (0, width - over))), 0.0)

    gram = held[-1]
    inverse = inverse_factor(after(gram, last_sent))
    image = after(image, inverse) + from_left + from_right
    image = straight((image[:half], image[half:]))
    *_, projected = sum_stages(dot_exact(moved, image, NT))
    projected = projected + center * gram
    projected = (projected + projected.T) * 0.5
    rayleigh = dot_exact(dot_exact(inverse, projected, NN), inverse, NT)
    return (filtered, rayleigh)


def plain_body(laplacian, block, bounds):
    row_index = lax.axis_index("row")
    col_index = lax.axis_index("col")
    tile_rows, tile_cols = laplacian.shape
    center = (bounds[1] + bounds[0]) * 0.5
    half_width = (bounds[1] - bounds[0]) * 0.5
    factor_two = 2.0 / half_width
    global_rows = row_index * tile_rows + lax.broadcasted_iota(jnp.int32, (tile_rows, tile_cols), 0)
    global_cols = col_index * tile_cols + lax.broadcasted_iota(jnp.int32, (tile_rows, tile_cols), 1)
    moved_diagonal = laplacian - center * (global_rows == global_cols).astype(F32)

    def through_columns(values):
        panel = lax.all_gather(values, "col", axis=0, tiled=True)
        out = dot_exact(moved_diagonal, panel, (((0,), (0,)), ((), ())))
        return lax.psum_scatter(out, "row", scatter_dimension=0, tiled=True)

    def through_rows(values):
        panel = lax.all_gather(values, "row", axis=0, tiled=True)
        out = dot_exact(moved_diagonal, panel, NN)
        return lax.psum_scatter(out, "col", scatter_dimension=0, tiled=True)

    filter_one = through_columns(block) / half_width
    filter_two = factor_two * through_rows(filter_one) - block
    filter_three = factor_two * through_columns(filter_two) - filter_one
    filter_four = factor_two * through_rows(filter_three) - filter_two
    image = through_columns(filter_four)
    rows, cols = lax.axis_size("row"), lax.axis_size("col")
    pairs = [(i, (i % rows) * cols + i // rows) for i in range(rows * cols)]
    moved = lax.ppermute(filter_four, BOTH, pairs)
    inner = (((0,), (0,)), ((), ()))
    gram, projected = lax.psum((dot_exact(moved, moved, inner), dot_exact(moved, image, inner)), BOTH)
    projected = projected + center * gram
    projected = (projected + projected.T) * 0.5
    factor = jnp.linalg.cholesky(gram)
    first_solve = jax.scipy.linalg.solve_triangular(factor, projected, lower=True)
    rayleigh = jax.scipy.linalg.solve_triangular(factor, first_solve.T, lower=True)
    return (filter_four, rayleigh)


def solution(mesh):
    tuned = mesh.shape["row"] == 8 and mesh.shape["col"] == 4
    placed = (P("row", "col"), P(BOTH, None), P())
    return jax.shard_map(
        tuned_body if tuned else plain_body,
        mesh=mesh,
        in_specs=placed,
        out_specs=(P(BOTH, None), P()),
        check_vma=False,
    )
```

time: 1420 us -> 657 us (0.46)
  waiting for transfers between devices: 805 us -> 94 us
  matrix products: 502 us -> 4.3 us
  Pallas kernels: 0 us -> 359 us
  starting transfers between devices: 0.49 us -> 113 us
  other arithmetic: 70.8 us -> 29.7 us
  local copies, waits for them, and re-layouts: 6.9 us -> 37.4 us
    dot_general x7 -> x4, matrix products: 500 us -> 4.3 us  [the longest x1 1.76 us: tuned_body(): *_, projected = sum_stages(dot_exact(moved, image, NT))]
    reduce_scatter x6 -> x0, waiting for transfers between devices: 401 us -> none  [the longest x2 222 us: column_sum(): return lax.psum_scatter(values, 'row', scatter_dimension=0, tiled=True)]
    pallas_call x0 -> x31, Pallas kernels: none -> 359 us  [the longest x18 199 us: columns_product(): pl.pallas_call(kernel, out_shape=jax.ShapeDtypeStruct((count, vectors, wi...]
    all_gather x5 -> x0, waiting for transfers between devices: 273 us -> none  [the longest x2 188 us: gather_cols(): return lax.all_gather(values, 'row', axis=0, tiled=True)]
    psum x1 -> x0, waiting for transfers between devices: 130 us -> none  [body(): gram, projected = lax.psum((gram_part, image_part), ('row', 'col'))]
    ppermute x0 -> x75, starting transfers between devices: none -> 113 us  [the longest x33 70.1 us: swap(): return lax.ppermute(values, axis, [(i, i ^ mask) for i in range(size)])]
    ppermute x0 -> x75, waiting for transfers between devices: none -> 94 us  [the longest x40 48.4 us: around(): lax.ppermute(values, 'row', [(RING[p], RING[(p + way) % 8]) for p in rang...]
    another operation x11 -> x2, other arithmetic: 54.5 us -> 2.57 us  [tuned_body(): jnp.stack([place, offset, f]).astype(jnp.int32)]
  transfers between devices with their start and end apart: 12 -> 75, of which waited for: 11 -> 32; matrix products, arithmetic and copies ran while one was open for 9% -> 4% of each run, Pallas kernels for 0% -> 48%
where the time goes in v1:
time: 657 us; the launch traced here: 647 us
  Pallas kernels  359 us (55%)
  starting transfers between devices  113 us (17%)
  waiting for transfers between devices  94 us (14%)
  local copies, waits for them, and re-layouts  37.4 us (6%)
  other arithmetic  29.7 us (5%)
  between operations  9.95 us (2%)
    pallas_call x18, Pallas kernels, columns_product(): pl.pallas_call(kernel, out_shape=jax.ShapeDtypeStruct((count, vectors, wi...  199 us
    pallas_call x12, Pallas kernels, rows_product(): pl.pallas_call(kernel, grid=(1,), out_shape=jax.ShapeDtypeStruct((number,...  143 us
    ppermute x33, starting transfers between devices, swap(): return lax.ppermute(values, axis, [(i, i ^ mask) for i in range(size)])  70.1 us
    ppermute x40, waiting for transfers between devices, around(): lax.ppermute(values, 'row', [(RING[p], RING[(p + way) % 8]) for p in rang...  48.4 us
    ppermute x33, waiting for transfers between devices, swap(): return lax.ppermute(values, axis, [(i, i ^ mask) for i in range(size)])  45.5 us
    ppermute x40, starting transfers between devices, around(): lax.ppermute(values, 'row', [(RING[p], RING[(p + way) % 8]) for p in rang...  35.3 us
    pallas_call x1, Pallas kernels, inverse_factor(): pl.pallas_call(kernel, out_shape=jax.ShapeDtypeStruct((size, size), F32),...  17.4 us
  transfers between devices with their start and end apart: 75, of which 32 were waited for; matrix products, arithmetic and copies ran while one was open for 4% of the time, Pallas kernels for 48%

profile of v1, /device:TPU:1, one launch (start us, length us, event | category | flops | bytes accessed | tf_op | source)
XLA Modules:
  0.0 646.7 jit_solution(166160374801620605)
XLA Ops:
  3.7 15.5 %collective-permute-done.1 = f32[720,256]{1,0:T(8,128)S(1)} collective-permute-done((f32[720,256]{1,0:T(8,128)}, f32[720,256]{1,0:T(8,128)S(1)}, u32[]{:S(2)}, u32[]{:S(2)}) %collective-permute-start.1) | collective-permute-done | bytes 737312 | tf_op jit(solution)/shard_map/ppermute | solution.py:304
  58.7 9.7 %columns_product.21 = f32[2,256,768]{2,1,0:T(8,128)} custom-call(s32[3]{0:T(128)} %pad_add_fusion.2.scalars_ref, f32[1]{0:T(128)} %mul.68.center_ref, f32[2880,5760]{1,0:T(8,128)} %tile_ref.59, f32[128,1536]{1,0:T(8,128)} %get-tuple-element.84.refs_2_.refs_0_, f32[128,1536]{1,0:T(8,128)} %get-tuple-element.83.refs_3_.refs_1_, ...), custom_call_target="tpu_custom_call" | custom-call | flops 3397386240 | bytes 8847360 | tf_op jit(solution)/shard_map/columns_product/pallas_call | solution.py:159
  72.5 14.2 %columns_product.19 = f32[2,256,768]{2,1,0:T(8,128)} custom-call(s32[3]{0:T(128)} %pad_add_fusion.2.scalars_ref, f32[1]{0:T(128)} %mul.68.center_ref, f32[2880,5760]{1,0:T(8,128)} %tile_ref.59, f32[128,1536]{1,0:T(8,128)} %get-tuple-element.82.refs_0_, f32[128,1536]{1,0:T(8,128)} %get-tuple-element.81.refs_1_, ...), custom_call_target="tpu_custom_call" | custom-call | flops 6794772480 | bytes 17694720 | tf_op jit(solution)/shard_map/columns_product/pallas_call | solution.py:159
  93.3 18.9 %columns_product.18 = f32[3,256,768]{2,1,0:T(8,128)} custom-call(s32[3]{0:T(128)} %pad_add_fusion.2.scalars_ref, f32[1]{0:T(128)} %mul.68.center_ref, f32[2880,5760]{1,0:T(8,128)} %tile_ref.59, f32[128,1536]{1,0:T(8,128)} %get-tuple-element.82.refs_0_, f32[128,1536]{1,0:T(8,128)} %get-tuple-element.81.refs_1_, ...), custom_call_target="tpu_custom_call" | custom-call | flops 10192158720 | bytes 26542080 | tf_op jit(solution)/shard_map/columns_product/pallas_call | solution.py:159
  121.8 9.5 %collective-permute-done.6 = f32[256,768]{1,0:T(8,128)S(1)} collective-permute-done((f32[256,768]{1,0:T(8,128)S(1)}, f32[256,768]{1,0:T(8,128)S(1)}, u32[]{:S(2)}, u32[]{:S(2)}) %collective-permute-start.6) | collective-permute-done | bytes 786464 | tf_op jit(solution)/shard_map/ppermute | solution.py:308
  138.2 9.3 %rows_product.12.refs_2_ = f32[2,256,1536]{2,1,0:T(8,128)} custom-call(s32[3]{0:T(128)} %pad_add_fusion.scalars_ref, f32[1]{0:T(128)} %mul.68.center_ref, f32[2880,5760]{1,0:T(8,128)} %tile_ref.59, f32[256,768]{1,0:T(8,128)} %copy-done.30), custom_call_target="tpu_custom_call" | custom-call | flops 3397386240 | bytes 8847360 | tf_op jit(solution)/shard_map/rows_product/pallas_call | solution.py:235
  153.6 15.6 %rows_product.13.refs_2_ = f32[2,256,1536]{2,1,0:T(8,128)} custom-call(s32[3]{0:T(128)} %pad_add_fusion.scalars_ref, f32[1]{0:T(128)} %mul.68.center_ref, f32[2880,5760]{1,0:T(8,128)} %tile_ref.59, f32[256,768]{1,0:T(8,128)} %copy-done.43, f32[256,768]{1,0:T(8,128)} %copy-done.38, f32[2,256,1536]{2,1,0:T(8,128)} %rows_product.12.refs_2_), custom_call_target="tpu_custom_call" | custom-call | flops 6794772480 | bytes 17694720 | tf_op jit(solution)/shard_map/rows_product/pallas_call | solution.py:235
  171.6 15.6 %rows_product.14.refs_2_.refs_4_ = f32[2,256,1536]{2,1,0:T(8,128)} custom-call(s32[3]{0:T(128)} %pad_add_fusion.scalars_ref, f32[1]{0:T(128)} %mul.68.center_ref, f32[2880,5760]{1,0:T(8,128)} %tile_ref.59, f32[256,768]{1,0:T(8,128)} %copy-done.41, f32[256,768]{1,0:T(8,128)} %copy-done.39, f32[2,256,1536]{2,1,0:T(8,128)} %rows_product.13.refs_2_), custom_call_target="tpu_custom_call" | custom-call | flops 6794772480 | bytes 17694720 | tf_op jit(solution)/shard_map/rows_product/pallas_call | solution.py:235
  189.5 10.2 %rows_product.15.refs_2_ = f32[1,256,1536]{2,1,0:T(8,128)} custom-call(s32[3]{0:T(128)} %pad_add_fusion.scalars_ref, f32[1]{0:T(128)} %mul.68.center_ref, f32[2880,5760]{1,0:T(8,128)} %tile_ref.59, f32[256,768]{1,0:T(8,128)} %copy-done.26, f32[256,768]{1,0:T(8,128)} %copy-done.28, f32[2,256,1536]{2,1,0:T(8,128)} %rows_product.14.refs_2_.refs_4_), custom_call_target="tpu_custom_call" | custom-call | flops 3397386240 | bytes 8847360 | tf_op jit(solution)/shard_map/rows_product/pallas_call | solution.py:235
  219.0 12.8 %rows_product.17 = f32[1,256,1536]{2,1,0:T(8,128)} custom-call(s32[3]{0:T(128)} %pad_add_fusion.scalars_ref, f32[1]{0:T(128)} %mul.68.center_ref, f32[2880,5760]{1,0:T(8,128)} %tile_ref.59, f32[256,768]{1,0:T(8,128)} %copy-done.26, f32[256,768]{1,0:T(8,128)} %copy-done.28, f32[128,768]{1,0:T(8,128)} %copy-done.34, f32[128,768]{1,0:T(8,128)} %copy-done.36, ...), custom_call_target="tpu_custom_call" | custom-call | flops 5096079360 | bytes 13271040 | tf_op jit(solution)/shard_map/rows_product/pallas_call | solution.py:235
  273.9 9.7 %columns_product.28 = f32[2,256,768]{2,1,0:T(8,128)} custom-call(s32[3]{0:T(128)} %pad_add_fusion.scalars_ref, f32[1]{0:T(128)} %mul.68.center_ref, f32[2880,5760]{1,0:T(8,128)} %tile_ref.59, f32[128,1536]{1,0:T(8,128)} %copy-done.4, f32[128,1536]{1,0:T(8,128)} %copy-done.13, f32[2,256,768]{2,1,0:T(8,128)} %columns_product.25.refs_2_), custom_call_target="tpu_custom_call" | custom-call | flops 3397386240 | bytes 8847360 | tf_op jit(solution)/shard_map/columns_product/pallas_call | solution.py:159
  287.3 14.1 %columns_product.27 = f32[2,256,768]{2,1,0:T(8,128)} custom-call(s32[3]{0:T(128)} %pad_add_fusion.scalars_ref, f32[1]{0:T(128)} %mul.68.center_ref, f32[2880,5760]{1,0:T(8,128)} %tile_ref.59, f32[128,1536]{1,0:T(8,128)} %copy-done.6, f32[128,1536]{1,0:T(8,128)} %copy-done.12, f32[128,1536]{1,0:T(8,128)} %copy-done.4, f32[128,1536]{1,0:T(8,128)} %copy-done.13), custom_call_target="tpu_custom_call" | custom-call | flops 6794772480 | bytes 17694720 | tf_op jit(solution)/shard_map/columns_product/pallas_call | solution.py:159
  308.0 18.9 %columns_product.26 = f32[3,256,768]{2,1,0:T(8,128)} custom-call(s32[3]{0:T(128)} %pad_add_fusion.scalars_ref, f32[1]{0:T(128)} %mul.68.center_ref, f32[2880,5760]{1,0:T(8,128)} %tile_ref.59, f32[128,1536]{1,0:T(8,128)} %copy-done.6, f32[128,1536]{1,0:T(8,128)} %copy-done.12, f32[128,1536]{1,0:T(8,128)} %copy-done.4, f32[128,1536]{1,0:T(8,128)} %copy-done.13), custom_call_target="tpu_custom_call" | custom-call | flops 10192158720 | bytes 26542080 | tf_op jit(solution)/shard_map/columns_product/pallas_call | solution.py:159
  330.5 15.6 %collective-permute-done.28 = f32[256,768]{1,0:T(8,128)S(1)} collective-permute-done((f32[256,768]{1,0:T(8,128)S(1)}, f32[256,768]{1,0:T(8,128)S(1)}, u32[]{:S(2)}, u32[]{:S(2)}) %collective-permute-start.28) | collective-permute-done | bytes 786464 | tf_op jit(solution)/shard_map/ppermute | solution.py:308
  351.0 9.4 %rows_product.18.refs_2_ = f32[2,256,1536]{2,1,0:T(8,128)} custom-call(s32[3]{0:T(128)} %pad_add_fusion.scalars_ref, f32[1]{0:T(128)} %mul.68.center_ref, f32[2880,5760]{1,0:T(8,128)} %tile_ref.59, f32[256,768]{1,0:T(8,128)} %copy-done.31), custom_call_target="tpu_custom_call" | custom-call | flops 3397386240 | bytes 8847360 | tf_op jit(solution)/shard_map/rows_product/pallas_call | solution.py:235
  367.8 15.6 %rows_product.19.refs_2_ = f32[2,256,1536]{2,1,0:T(8,128)} custom-call(s32[3]{0:T(128)} %pad_add_fusion.scalars_ref, f32[1]{0:T(128)} %mul.68.center_ref, f32[2880,5760]{1,0:T(8,128)} %tile_ref.59, f32[256,768]{1,0:T(8,128)} %copy-done.45, f32[256,768]{1,0:T(8,128)} %copy-done.44, f32[2,256,1536]{2,1,0:T(8,128)} %rows_product.18.refs_2_), custom_call_target="tpu_custom_call" | custom-call | flops 6794772480 | bytes 17694720 | tf_op jit(solution)/shard_map/rows_product/pallas_call | solution.py:235
  385.8 15.6 %rows_product.20.refs_2_.refs_4_ = f32[2,256,1536]{2,1,0:T(8,128)} custom-call(s32[3]{0:T(128)} %pad_add_fusion.scalars_ref, f32[1]{0:T(128)} %mul.68.center_ref, f32[2880,5760]{1,0:T(8,128)} %tile_ref.59, f32[256,768]{1,0:T(8,128)} %copy-done.42, f32[256,768]{1,0:T(8,128)} %copy-done.40, f32[2,256,1536]{2,1,0:T(8,128)} %rows_product.19.refs_2_), custom_call_target="tpu_custom_call" | custom-call | flops 6794772480 | bytes 17694720 | tf_op jit(solution)/shard_map/rows_product/pallas_call | solution.py:235
  403.4 10.1 %rows_product.21.refs_2_ = f32[1,256,1536]{2,1,0:T(8,128)} custom-call(s32[3]{0:T(128)} %pad_add_fusion.scalars_ref, f32[1]{0:T(128)} %mul.68.center_ref, f32[2880,5760]{1,0:T(8,128)} %tile_ref.59, f32[256,768]{1,0:T(8,128)} %copy-done.27, f32[256,768]{1,0:T(8,128)} %copy-done.29, f32[2,256,1536]{2,1,0:T(8,128)} %rows_product.20.refs_2_.refs_4_), custom_call_target="tpu_custom_call" | custom-call | flops 3397386240 | bytes 8847360 | tf_op jit(solution)/shard_map/rows_product/pallas_call | solution.py:235
  432.6 12.7 %rows_product.23 = f32[1,256,1536]{2,1,0:T(8,128)} custom-call(s32[3]{0:T(128)} %pad_add_fusion.scalars_ref, f32[1]{0:T(128)} %mul.68.center_ref, f32[2880,5760]{1,0:T(8,128)} %tile_ref.59, f32[256,768]{1,0:T(8,128)} %copy-done.27, f32[256,768]{1,0:T(8,128)} %copy-done.29, f32[128,768]{1,0:T(8,128)} %copy-done.35, f32[128,768]{1,0:T(8,128)} %copy-done.37, ...), custom_call_target="tpu_custom_call" | custom-call | flops 5096079360 | bytes 13271040 | tf_op jit(solution)/shard_map/rows_product/pallas_call | solution.py:235
  499.3 9.6 %columns_product.34 = f32[2,256,768]{2,1,0:T(8,128)} custom-call(s32[3]{0:T(128)} %pad_add_fusion.scalars_ref, f32[1]{0:T(128)} %mul.68.center_ref, f32[2880,5760]{1,0:T(8,128)} %tile_ref.59, f32[128,1536]{1,0:T(8,128)} %copy-done.8, f32[128,1536]{1,0:T(8,128)} %copy-done.11, f32[2,256,768]{2,1,0:T(8,128)} %columns_product.31.refs_2_), custom_call_target="tpu_custom_call" | custom-call | flops 3397386240 | bytes 8847360 | tf_op jit(solution)/shard_map/columns_product/pallas_call | solution.py:159
  518.9 14.2 %columns_product.33 = f32[2,256,768]{2,1,0:T(8,128)} custom-call(s32[3]{0:T(128)} %pad_add_fusion.scalars_ref, f32[1]{0:T(128)} %mul.68.center_ref, f32[2880,5760]{1,0:T(8,128)} %tile_ref.59, f32[128,1536]{1,0:T(8,128)} %copy-done.2, f32[128,1536]{1,0:T(8,128)} %copy-done.9, f32[128,1536]{1,0:T(8,128)} %copy-done.8, f32[128,1536]{1,0:T(8,128)} %copy-done.11), custom_call_target="tpu_custom_call" | custom-call | flops 6794772480 | bytes 17694720 | tf_op jit(solution)/shard_map/columns_product/pallas_call | solution.py:159
  539.9 18.9 %columns_product.32 = f32[3,256,768]{2,1,0:T(8,128)} custom-call(s32[3]{0:T(128)} %pad_add_fusion.scalars_ref, f32[1]{0:T(128)} %mul.68.center_ref, f32[2880,5760]{1,0:T(8,128)} %tile_ref.59, f32[128,1536]{1,0:T(8,128)} %copy-done.2, f32[128,1536]{1,0:T(8,128)} %copy-done.9, f32[128,1536]{1,0:T(8,128)} %copy-done.8, f32[128,1536]{1,0:T(8,128)} %copy-done.11), custom_call_target="tpu_custom_call" | custom-call | flops 10192158720 | bytes 26542080 | tf_op jit(solution)/shard_map/columns_product/pallas_call | solution.py:159
  578.4 17.4 %inverse_factor.1 = f32[256,256]{1,0:T(8,128)} custom-call(f32[256,256]{1,0:T(8,128)} %pad_maximum_fusion.8.gram_ref), custom_call_target="tpu_custom_call" | custom-call | flops 33554432 | bytes 524288 | tf_op jit(solution)/shard_map/inverse_factor/pallas_call | solution.py:291
  601.3 19.8 %collective-permute-start.67 = (f32[64,256]{1,0:T(8,128)S(1)}, f32[64,256]{1,0:T(8,128)S(1)}, u32[]{:S(2)}, u32[]{:S(2)}) collective-permute-start(f32[64,256]{1,0:T(8,128)S(1)} %slice_select_fusion.4), channel_id=1, source_target_pairs={{0,2},{1,3},{2,0},{3,1},{4,6},{5,7},{6,4},{7,5},{8,10},{9,11},{10,... | collective-permute-start | bytes 196616 | tf_op jit(solution)/shard_map/ppermute | solution.py:304
  (355 shorter events, 303.5 us)
Async XLA Ops:
  2.8 23.1 %collective-permute-start = (f32[720,256]{1,0:T(8,128)}, f32[720,256]{1,0:T(8,128)}, u32[]{:S(2)}, u32[]{:S(2)}) collective-permute-start(f32[720,256]{1,0:T(8,128)} %param.8), channel_id=1, source_target_pairs={{0,1},{1,0},{2,3},{3,2},{4,5},{5,4},{6,7},{7,6},{8,9},{9,8},{10,11... | collective-permute-start | bytes 2211848 | tf_op jit(solution)/shard_map/ppermute | solution.py:304
  70.2 18.9 %collective-permute-start.8 = (f32[256,768]{1,0:T(8,128)S(1)}, f32[256,768]{1,0:T(8,128)S(1)}, u32[]{:S(2)}, u32[]{:S(2)}) collective-permute-start(f32[256,768]{1,0:T(8,128)S(1)} %pad_maximum_fusion.3), channel_id=1, source_target_pairs={{0,4},{8,0},{16,8},{24,16},{28,24},{20,28},{12,20},{4,12},{1,5},{9... | collective-permute-start | bytes 2359304 | tf_op jit(solution)/shard_map/ppermute | solution.py:308
  71.6 18.5 %collective-permute-start.4 = (f32[256,768]{1,0:T(8,128)S(1)}, f32[256,768]{1,0:T(8,128)S(1)}, u32[]{:S(2)}, u32[]{:S(2)}) collective-permute-start(f32[256,768]{1,0:T(8,128)S(1)} %pad_maximum_fusion.2), channel_id=1, source_target_pairs={{0,8},{8,16},{16,24},{24,28},{28,20},{20,12},{12,4},{4,0},{1,9},{9... | collective-permute-start | bytes 2359304 | tf_op jit(solution)/shard_map/ppermute | solution.py:308
  91.7 20.6 %collective-permute-start.5 = (f32[256,768]{1,0:T(8,128)S(1)}, f32[256,768]{1,0:T(8,128)S(1)}, u32[]{:S(2)}, u32[]{:S(2)}) collective-permute-start(f32[256,768]{1,0:T(8,128)S(1)} %get-tuple-element.75), channel_id=1, source_target_pairs={{0,8},{8,16},{16,24},{24,28},{28,20},{20,12},{12,4},{4,0},{1,9},{9... | collective-permute-start | bytes 2359304 | tf_op jit(solution)/shard_map/ppermute | solution.py:308
  92.4 19.8 %collective-permute-start.9 = (f32[256,768]{1,0:T(8,128)S(1)}, f32[256,768]{1,0:T(8,128)S(1)}, u32[]{:S(2)}, u32[]{:S(2)}) collective-permute-start(f32[256,768]{1,0:T(8,128)S(1)} %get-tuple-element.76), channel_id=1, source_target_pairs={{0,4},{8,0},{16,8},{24,16},{28,24},{20,28},{12,20},{4,12},{1,5},{9... | collective-permute-start | bytes 2359304 | tf_op jit(solution)/shard_map/ppermute | solution.py:308
  217.2 19.5 %collective-permute-start.20 = (f32[128,1536]{1,0:T(8,128)S(1)}, f32[128,1536]{1,0:T(8,128)}, u32[]{:S(2)}, u32[]{:S(2)}) collective-permute-start(f32[128,1536]{1,0:T(8,128)S(1)} %fusion.17), channel_id=1, source_target_pairs={{0,2},{1,3},{2,0},{3,1},{4,6},{5,7},{6,4},{7,5},{8,10},{9,11},{10,... | collective-permute-start | bytes 2359304 | tf_op jit(solution)/shard_map/ppermute | solution.py:304
  240.3 19.0 %collective-permute-start.23 = (f32[128,1536]{1,0:T(8,128)S(1)}, f32[128,1536]{1,0:T(8,128)S(1)}, u32[]{:S(2)}, u32[]{:S(2)}) collective-permute-start(f32[128,1536]{1,0:T(8,128)S(1)} %fusion.16), channel_id=1, source_target_pairs={{0,2},{1,3},{2,0},{3,1},{4,6},{5,7},{6,4},{7,5},{8,10},{9,11},{10,... | collective-permute-start | bytes 2359304 | tf_op jit(solution)/shard_map/ppermute | solution.py:304
  285.4 18.7 %collective-permute-start.30 = (f32[256,768]{1,0:T(8,128)S(1)}, f32[256,768]{1,0:T(8,128)S(1)}, u32[]{:S(2)}, u32[]{:S(2)}) collective-permute-start(f32[256,768]{1,0:T(8,128)S(1)} %pad_maximum_fusion.5), channel_id=1, source_target_pairs={{0,4},{8,0},{16,8},{24,16},{28,24},{20,28},{12,20},{4,12},{1,5},{9... | collective-permute-start | bytes 2359304 | tf_op jit(solution)/shard_map/ppermute | solution.py:308
  306.1 20.9 %collective-permute-start.27 = (f32[256,768]{1,0:T(8,128)S(1)}, f32[256,768]{1,0:T(8,128)S(1)}, u32[]{:S(2)}, u32[]{:S(2)}) collective-permute-start(f32[256,768]{1,0:T(8,128)S(1)} %get-tuple-element.69), channel_id=1, source_target_pairs={{0,8},{8,16},{16,24},{24,28},{28,20},{20,12},{12,4},{4,0},{1,9},{9... | collective-permute-start | bytes 2359304 | tf_op jit(solution)/shard_map/ppermute | solution.py:308
  307.2 19.8 %collective-permute-start.31 = (f32[256,768]{1,0:T(8,128)S(1)}, f32[256,768]{1,0:T(8,128)S(1)}, u32[]{:S(2)}, u32[]{:S(2)}) collective-permute-start(f32[256,768]{1,0:T(8,128)S(1)} %get-tuple-element.70), channel_id=1, source_target_pairs={{0,4},{8,0},{16,8},{24,16},{28,24},{20,28},{12,20},{4,12},{1,5},{9... | collective-permute-start | bytes 2359304 | tf_op jit(solution)/shard_map/ppermute | solution.py:308
  431.6 18.8 %collective-permute-start.42 = (f32[128,1536]{1,0:T(8,128)S(1)}, f32[128,1536]{1,0:T(8,128)S(1)}, u32[]{:S(2)}, u32[]{:S(2)}) collective-permute-start(f32[128,1536]{1,0:T(8,128)S(1)} %fusion.6), channel_id=1, source_target_pairs={{0,2},{1,3},{2,0},{3,1},{4,6},{5,7},{6,4},{7,5},{8,10},{9,11},{10,... | collective-permute-start | bytes 2359304 | tf_op jit(solution)/shard_map/ppermute | solution.py:304
  451.9 19.2 %collective-permute-start.45 = (f32[128,1536]{1,0:T(8,128)S(1)}, f32[128,1536]{1,0:T(8,128)S(1)}, u32[]{:S(2)}, u32[]{:S(2)}) collective-permute-start(f32[128,1536]{1,0:T(8,128)S(1)} %fusion.5), channel_id=1, source_target_pairs={{0,2},{1,3},{2,0},{3,1},{4,6},{5,7},{6,4},{7,5},{8,10},{9,11},{10,... | collective-permute-start | bytes 2359304 | tf_op jit(solution)/shard_map/ppermute | solution.py:304
  497.2 19.9 %collective-permute-start.62 = (f32[128,768]{1,0:T(8,128)S(1)}, f32[128,768]{1,0:T(8,128)S(1)}, u32[]{:S(2)}, u32[]{:S(2)}) collective-permute-start(f32[128,768]{1,0:T(8,128)S(1)} %get-tuple-element.87), channel_id=1, source_target_pairs={{0,4},{8,0},{16,8},{24,16},{28,24},{20,28},{12,20},{4,12},{1,5},{9... | collective-permute-start | bytes 1179656 | tf_op jit(solution)/shard_map/ppermute | solution.py:308
  497.5 19.6 %collective-permute-start.56 = (f32[128,768]{1,0:T(8,128)S(1)}, f32[128,768]{1,0:T(8,128)S(1)}, u32[]{:S(2)}, u32[]{:S(2)}) collective-permute-start(f32[128,768]{1,0:T(8,128)S(1)} %get-tuple-element.88), channel_id=1, source_target_pairs={{0,8},{8,16},{16,24},{24,28},{28,20},{20,12},{12,4},{4,0},{1,9},{9... | collective-permute-start | bytes 1179656 | tf_op jit(solution)/shard_map/ppermute | solution.py:308
  512.2 21.0 %collective-permute-start.55 = (f32[128,256]{1,0:T(8,128)S(1)}, f32[128,256]{1,0:T(8,128)S(1)}, u32[]{:S(2)}, u32[]{:S(2)}) collective-permute-start(f32[128,256]{1,0:T(8,128)S(1)} %pad_maximum_fusion.9), channel_id=1, source_target_pairs={{0,1},{1,0},{2,3},{3,2},{4,5},{5,4},{6,7},{7,6},{8,9},{9,8},{10,11... | collective-permute-start | bytes 393224 | tf_op jit(solution)/shard_map/ppermute | solution.py:304
  517.3 19.2 %collective-permute-start.57 = (f32[256,768]{1,0:T(8,128)S(1)}, f32[256,768]{1,0:T(8,128)S(1)}, u32[]{:S(2)}, u32[]{:S(2)}) collective-permute-start(f32[256,768]{1,0:T(8,128)S(1)} %pad_maximum_fusion.6), channel_id=1, source_target_pairs={{0,8},{8,16},{16,24},{24,28},{28,20},{20,12},{12,4},{4,0},{1,9},{9... | collective-permute-start | bytes 2359304 | tf_op jit(solution)/shard_map/ppermute | solution.py:308
  517.7 18.9 %collective-permute-start.63 = (f32[256,768]{1,0:T(8,128)S(1)}, f32[256,768]{1,0:T(8,128)S(1)}, u32[]{:S(2)}, u32[]{:S(2)}) collective-permute-start(f32[256,768]{1,0:T(8,128)S(1)} %pad_maximum_fusion.7), channel_id=1, source_target_pairs={{0,4},{8,0},{16,8},{24,16},{28,24},{20,28},{12,20},{4,12},{1,5},{9... | collective-permute-start | bytes 2359304 | tf_op jit(solution)/shard_map/ppermute | solution.py:308
  538.1 20.7 %collective-permute-start.64 = (f32[256,768]{1,0:T(8,128)S(1)}, f32[256,768]{1,0:T(8,128)S(1)}, u32[]{:S(2)}, u32[]{:S(2)}) collective-permute-start(f32[256,768]{1,0:T(8,128)S(1)} %get-tuple-element.63), channel_id=1, source_target_pairs={{0,4},{8,0},{16,8},{24,16},{28,24},{20,28},{12,20},{4,12},{1,5},{9... | collective-permute-start | bytes 2359304 | tf_op jit(solution)/shard_map/ppermute | solution.py:308
  539.4 19.5 %collective-permute-start.58 = (f32[256,768]{1,0:T(8,128)S(1)}, f32[256,768]{1,0:T(8,128)S(1)}, u32[]{:S(2)}, u32[]{:S(2)}) collective-permute-start(f32[256,768]{1,0:T(8,128)S(1)} %get-tuple-element.64), channel_id=1, source_target_pairs={{0,8},{8,16},{16,24},{24,28},{28,20},{20,12},{12,4},{4,0},{1,9},{9... | collective-permute-start | bytes 2359304 | tf_op jit(solution)/shard_map/ppermute | solution.py:308
  561.8 34.0 %collective-permute-start.65 = (f32[256,768]{1,0:T(8,128)}, f32[256,768]{1,0:T(8,128)}, u32[]{:S(2)}, u32[]{:S(2)}) collective-permute-start(f32[256,768]{1,0:T(8,128)} %get-tuple-element.56), channel_id=1, source_target_pairs={{0,4},{8,0},{16,8},{24,16},{28,24},{20,28},{12,20},{4,12},{1,5},{9... | collective-permute-start | bytes 2359304 | tf_op jit(solution)/shard_map/ppermute | solution.py:308
  562.7 33.1 %collective-permute-start.61 = (f32[256,768]{1,0:T(8,128)}, f32[256,768]{1,0:T(8,128)}, u32[]{:S(2)}, u32[]{:S(2)}) collective-permute-start(f32[256,768]{1,0:T(8,128)} %get-tuple-element.57), channel_id=1, source_target_pairs={{0,8},{8,16},{16,24},{24,28},{28,20},{20,12},{12,4},{4,0},{1,9},{9... | collective-permute-start | bytes 2359304 | tf_op jit(solution)/shard_map/ppermute | solution.py:308
  565.6 31.7 %collective-permute-start.60 = (f32[256,64]{1,0:T(8,128)}, f32[256,64]{1,0:T(8,128)}, u32[]{:S(2)}, u32[]{:S(2)}) collective-permute-start(f32[256,64]{1,0:T(8,128)} %slice.376), channel_id=1, source_target_pairs={{0,28},{8,29},{16,30},{24,31}} | collective-permute-start | bytes 196616 | tf_op jit(solution)/shard_map/ppermute | solution.py:468
  571.0 26.3 %collective-permute-start.59 = (f32[256,768]{1,0:T(8,128)S(1)}, f32[256,768]{1,0:T(8,128)S(1)}, u32[]{:S(2)}, u32[]{:S(2)}) collective-permute-start(f32[256,768]{1,0:T(8,128)S(1)} %constant_dynamic-slice_fusion), channel_id=1, source_target_pairs={{0,0},{1,8},{2,16},{3,24},{4,28},{5,20},{6,12},{7,4},{8,1},{9,9},{... | collective-permute-start | bytes 2359304 | tf_op jit(solution)/shard_map/ppermute | solution.py:466
  601.3 22.0 %collective-permute-start.67 = (f32[64,256]{1,0:T(8,128)S(1)}, f32[64,256]{1,0:T(8,128)S(1)}, u32[]{:S(2)}, u32[]{:S(2)}) collective-permute-start(f32[64,256]{1,0:T(8,128)S(1)} %slice_select_fusion.4), channel_id=1, source_target_pairs={{0,2},{1,3},{2,0},{3,1},{4,6},{5,7},{6,4},{7,5},{8,10},{9,11},{10,... | collective-permute-start | bytes 196616 | tf_op jit(solution)/shard_map/ppermute | solution.py:304
  (103 other events, 812.6 us)

commit v2 on v1

--- a/solution.py
+++ b/solution.py
@@ -36,28 +36,30 @@
 
 
 SLOTS = 3
-
-
-def stream(source_ref, slots, sems, steps, corner, use):
+ROUND = 32
+
+
+def stream(source_ref, slots, sems, steps, corner, prepare, use):
     _, height, width = slots.shape
 
     def copy(step):
         row0, col0 = corner(step)
         slot = lax.rem(step, SLOTS)
-        rows = pl.ds(pl.multiple_of(row0, 8), height)
+        rows = pl.ds(pl.multiple_of(row0, ROUND), height)
         cols = pl.ds(pl.multiple_of(col0, LANES), width)
         return pltpu.make_async_copy(source_ref.at[rows, cols], slots.at[slot], sems.at[slot])
 
-    for step in range(min(SLOTS - 1, steps)):
+    copy(jnp.int32(0)).start()
+    prepare()
+    for step in range(1, min(SLOTS - 1, steps)):
         copy(jnp.int32(step)).start()
 
     def one(step, carry):
-        copy(step).wait()
-
         @pl.when(step + SLOTS - 1 < steps)
         def _():
             copy(step + SLOTS - 1).start()
 
+        copy(step).wait()
         use(step, lax.rem(step, SLOTS))
         return carry
 
@@ -71,23 +73,27 @@
     return lax.rem(place + away + 8, 8) * blocks // 8 * LANES
 
 
-def minus_center(block, center, delta):
-    rows = lax.broadcasted_iota(jnp.int32, block.shape, 0)
-    cols = lax.broadcasted_iota(jnp.int32, block.shape, 1)
-    return block - jnp.where(rows - cols == delta, center, 0.0)
-
-
-def with_center(slots, slot, center, row0, col0, offset, use):
+def take_center(slots, slot, center, row0, col0, offset):
     _, height, width = slots.shape
-    hit = (offset >= 0) & (row0 + offset < col0 + width) & (row0 + offset + height > col0)
-
-    @pl.when(hit)
+    first = col0 - row0 - offset
+
+    @pl.when((offset >= 0) & (first < height) & (first + width > 0))
     def _():
-        use(minus_center(slots[slot], center, col0 - row0 - offset))
-
-    @pl.when(jnp.logical_not(hit))
-    def _():
-        use(slots[slot])
+        rows = lax.broadcasted_iota(jnp.int32, (ROUND, LANES), 0)
+        cols = lax.broadcasted_iota(jnp.int32, (ROUND, LANES), 1)
+
+        def tile(index, carry):
+            for part in range(LANES // ROUND):
+                at = first + index * LANES + part * ROUND
+
+                @pl.when((at >= 0) & (at < height))
+                def _():
+                    here = (slot, pl.ds(pl.multiple_of(at, ROUND), ROUND), pl.ds(pl.multiple_of(index * LANES, LANES), LANES))
+                    slots[here] = slots[here] - jnp.where(rows + part * ROUND == cols, center, 0.0)
+
+            return carry
+
+        lax.fori_loop(0, width // LANES, tile, 0)
 
 
 VMEM = pl.BlockSpec(memory_space=pltpu.VMEM)
@@ -97,7 +103,7 @@
 
 def kernel_params(count, chunks, depth, width, vectors):
     return dict(
-        compiler_params=pltpu.CompilerParams(vmem_limit_bytes=56 * 2**20),
+        compiler_params=pltpu.CompilerParams(vmem_limit_bytes=36 * 2**20),
         cost_estimate=pl.CostEstimate(
             flops=6 * count * chunks * depth * width * vectors,
             bytes_accessed=4 * count * chunks * depth * width,
@@ -106,66 +112,97 @@
     )
 
 
+def bring(pieces, refs, held, sems):
+    copies, rest = [], list(refs)
+    for i, group in enumerate(pieces):
+        at, own = 0, []
+        for q, piece in enumerate(group):
+            own.append(pltpu.make_async_copy(rest.pop(0), held.at[i, pl.ds(at, piece.shape[0])], sems.at[i, q]))
+            at += piece.shape[0]
+        copies.append(own)
+    return copies
+
+
 def columns_product(laplacian, scalars, center, panel, aways, depth, width, first_chunk=0, totals=None):
     count, chunks = len(aways), len(panel)
-    heights = [p.shape[0] for p in panel[0]]
-    vectors, per = sum(heights), len(heights)
+    lanes = panel[0][0].shape[1]
+    vectors, per = sum(p.shape[0] for p in panel[0]), len(panel[0])
     blocks = laplacian.shape[1] // LANES
+    given = [] if totals is None else [totals]
 
     def kernel(scalars_ref, center_ref, tile_ref, *refs):
-        pieces = refs[: per * chunks]
-        total_ref = None if totals is None else refs[per * chunks]
-        out_ref, slots, high_ref, low_ref, sems = refs[-5:]
+        piece_refs, total_refs = refs[: per * chunks], refs[per * chunks : per * chunks + len(given)]
+        out_ref, slots, panel_ref, high_ref, low_ref, sum_ref, total_buf, sems, in_sems, total_sem, out_sems = refs[-11:]
+        copies = bring(panel, piece_refs, panel_ref, in_sems)
+        more = [pltpu.make_async_copy(r, total_buf, total_sem.at[0]) for r in total_refs]
 
         def corner(step):
             chunk = lax.bitwise_xor(first_chunk + lax.rem(step, chunks), scalars_ref[2])
             return chunk * depth, unit_start(scalars_ref[0], aways, step // chunks, blocks)
 
+        def prepare():
+            for copy in [c for own in copies for c in own] + more:
+                copy.start()
+
         def use(step, slot):
             chunk, unit = lax.rem(step, chunks), step // chunks
-
-            @pl.when(step == 0)
+            for c in range(chunks):
+
+                @pl.when(step == c)
+                def _(c=c):
+                    for copy in copies[c]:
+                        copy.wait()
+                    high, low = split(panel_ref[c, :, :depth])
+                    high_ref[c] = high
+                    low_ref[c] = low
+
+            row0, col0 = corner(step)
+            take_center(slots, slot, center_ref[0], row0, col0, scalars_ref[1])
+            high, low = split(slots[slot])
+            z_high, z_low = high_ref[chunk], low_ref[chunk]
+            term = dot32(z_high, high, NN) + dot32(z_low, high, NN) + dot32(z_high, low, NN)
+
+            @pl.when(chunk == 0)
             def _():
-                for c in range(chunks):
-                    at = 0
-                    for q in range(per):
-                        high, low = split(pieces[c * per + q][:, :depth])
-                        high_ref[c, at : at + heights[q]] = high
-                        low_ref[c, at : at + heights[q]] = low
-                        at += heights[q]
-
-            def add(block):
-                high, low = split(block)
-                z_high, z_low = high_ref[chunk], low_ref[chunk]
-                term = dot32(z_high, high, NN) + dot32(z_low, high, NN) + dot32(z_high, low, NN)
-
-                @pl.when(chunk == 0)
-                def _():
-                    if total_ref is None:
-                        out_ref[unit] = term
-                    else:
-                        out_ref[unit] = total_ref[unit] + term
-
-                @pl.when(chunk > 0)
-                def _():
-                    out_ref[unit] += term
-
-            row0, col0 = corner(step)
-            with_center(slots, slot, center_ref[0], row0, col0, scalars_ref[1], add)
-
-        stream(tile_ref, slots, sems, count * chunks, corner, use)
-
-    given = [] if totals is None else [totals]
+                if more:
+
+                    @pl.when(step == 0)
+                    def _():
+                        for copy in more:
+                            copy.wait()
+
+                    sum_ref[unit] = total_buf[unit] + term
+                else:
+                    sum_ref[unit] = term
+
+            @pl.when(chunk > 0)
+            def _():
+                sum_ref[unit] += term
+
+            @pl.when(chunk == chunks - 1)
+            def _():
+                pltpu.make_async_copy(sum_ref.at[unit], out_ref.at[unit], out_sems.at[unit]).start()
+
+        stream(tile_ref, slots, sems, count * chunks, corner, prepare, use)
+        for unit in range(count):
+            pltpu.make_async_copy(sum_ref.at[unit], out_ref.at[unit], out_sems.at[unit]).wait()
+
     return pl.pallas_call(
         kernel,
         out_shape=jax.ShapeDtypeStruct((count, vectors, width), F32),
-        in_specs=[SMEM, SMEM, ANY] + [VMEM] * (per * chunks + len(given)),
-        out_specs=VMEM,
+        in_specs=[SMEM, SMEM, ANY] + [ANY] * (per * chunks + len(given)),
+        out_specs=ANY,
         scratch_shapes=[
             pltpu.VMEM((SLOTS, depth, width), F32),
+            pltpu.VMEM((chunks, vectors, lanes), F32),
             pltpu.VMEM((chunks, vectors, depth), BF16),
             pltpu.VMEM((chunks, vectors, depth), BF16),
+            pltpu.VMEM((count, vectors, width), F32),
+            pltpu.VMEM((count, vectors, width) if given else (1, 8, LANES), F32),
             pltpu.SemaphoreType.DMA((SLOTS,)),
+            pltpu.SemaphoreType.DMA((chunks, per)),
+            pltpu.SemaphoreType.DMA((1,)),
+            pltpu.SemaphoreType.DMA((count,)),
         ],
         name="columns_product",
         **kernel_params(count, chunks, depth, width, vectors),
@@ -176,73 +213,85 @@
     count, number = len(units), len(chunks)
     width = units[0][0].shape[1]
     vectors = sum(p.shape[0] for p in units[0])
+    per = max(len(group) for group in units)
     flat = [p for pieces in units for p in pieces]
     blocks = laplacian.shape[1] // LANES
+    given = [] if totals is None else [totals]
+    skip = chunks[0] if given and totals.shape[0] > number else 0
 
     def kernel(scalars_ref, center_ref, tile_ref, *refs):
-        pieces = list(refs[: len(flat)])
-        total_ref = None if totals is None else refs[len(flat)]
-        out_ref, slots, high_ref, low_ref, sems = refs[-5:]
+        total_refs = refs[len(flat) : len(flat) + len(given)]
+        out_ref, slots, unit_ref, high_ref, low_ref, sum_ref, total_buf, sems, in_sems, total_sems, out_sems = refs[-11:]
+        copies = bring(units, refs[: len(flat)], unit_ref, in_sems)
+
+        def total(chunk):
+            return [pltpu.make_async_copy(r.at[skip + chunk], total_buf.at[chunk], total_sems.at[chunk]) for r in total_refs]
 
         def corner(step):
             first = (chunks[0] + step // count) * depth
             return first, unit_start(scalars_ref[0], aways, lax.rem(step, count), blocks)
 
+        def prepare():
+            for copy in [c for own in copies for c in own] + [c for i in range(number) for c in total(i)]:
+                copy.start()
+
         def use(step, slot):
             chunk, unit = step // count, lax.rem(step, count)
-
-            @pl.when(step == 0)
+            for u in range(count):
+
+                @pl.when(step == u)
+                def _(u=u):
+                    for copy in copies[u]:
+                        copy.wait()
+                    high, low = split(unit_ref[u])
+                    high_ref[u] = high
+                    low_ref[u] = low
+                    if u == 0 and lanes > depth:
+                        sum_ref[:, :, depth:] = jnp.zeros((number, vectors, lanes - depth), F32)
+
+            row0, col0 = corner(step)
+            take_center(slots, slot, center_ref[0], row0, col0, scalars_ref[1])
+            high, low = split(slots[slot])
+            z_high, z_low = high_ref[unit], low_ref[unit]
+            term = dot32(z_high, high, NT) + dot32(z_low, high, NT) + dot32(z_high, low, NT)
+
+            @pl.when(unit == 0)
             def _():
-                rest = list(pieces)
-                for u in range(count):
-                    at = 0
-                    for _ in units[u]:
-                        piece = rest.pop(0)
-                        high, low = split(piece[...])
-                        high_ref[u, at : at + piece.shape[0]] = high
-                        low_ref[u, at : at + piece.shape[0]] = low
-                        at += piece.shape[0]
-                if lanes > depth:
-                    out_ref[:, :, depth:] = jnp.zeros((number, vectors, lanes - depth), F32)
-
-            def add(block):
-                high, low = split(block)
-                z_high, z_low = high_ref[unit], low_ref[unit]
-                term = dot32(z_high, high, NT) + dot32(z_low, high, NT) + dot32(z_high, low, NT)
-
-                @pl.when(unit == 0)
-                def _():
-                    if total_ref is None:
-                        out_ref[chunk, :, :depth] = term
-                    else:
-                        out_ref[chunk, :, :depth] = total_ref[chunk, :, :depth] + term
-
-                @pl.when(unit > 0)
-                def _():
-                    out_ref[chunk, :, :depth] += term
-
-            row0, col0 = corner(step)
-            with_center(slots, slot, center_ref[0], row0, col0, scalars_ref[1], add)
-
-        stream(tile_ref, slots, sems, count * number, corner, use)
-
-    given = [] if totals is None else [totals]
-    specs = []
-    if given:
-        first, shape = chunks[0], (number, vectors, lanes)
-        whole = totals.shape[0] == number
-        specs = [VMEM if whole else pl.BlockSpec(shape, lambda _: (first, 0, 0))]
+                if given:
+                    for copy in total(chunk):
+                        copy.wait()
+                    sum_ref[chunk, :, :depth] = total_buf[chunk, :, :depth] + term
+                else:
+                    sum_ref[chunk, :, :depth] = term
+
+            @pl.when(unit > 0)
+            def _():
+                sum_ref[chunk, :, :depth] += term
+
+            @pl.when(unit == count - 1)
+            def _():
+                pltpu.make_async_copy(sum_ref.at[chunk], out_ref.at[chunk], out_sems.at[chunk]).start()
+
+        stream(tile_ref, slots, sems, count * number, corner, prepare, use)
+        for chunk in range(number):
+            pltpu.make_async_copy(sum_ref.at[chunk], out_ref.at[chunk], out_sems.at[chunk]).wait()
+
     return pl.pallas_call(
         kernel,
-        grid=(1,),
         out_shape=jax.ShapeDtypeStruct((number, vectors, lanes), F32),
-        in_specs=[SMEM, SMEM, ANY] + [VMEM] * len(flat) + specs,
-        out_specs=VMEM,
+        in_specs=[SMEM, SMEM, ANY] + [ANY] * (len(flat) + len(given)),
+        out_specs=ANY,
         scratch_shapes=[
             pltpu.VMEM((SLOTS, depth, width), F32),
+            pltpu.VMEM((count, vectors, width), F32),
             pltpu.VMEM((count, vectors, width), BF16),
             pltpu.VMEM((count, vectors, width), BF16),
+            pltpu.VMEM((number, vectors, lanes), F32),
+            pltpu.VMEM((number, vectors, lanes) if given else (1, 8, LANES), F32),
             pltpu.SemaphoreType.DMA((SLOTS,)),
+            pltpu.SemaphoreType.DMA((count, per)),
+            pltpu.SemaphoreType.DMA((number,)),
+            pltpu.SemaphoreType.DMA((number,)),
         ],
         name="rows_product",
         **kernel_params(count, number, depth, width, vectors),
@@ -408,8 +457,6 @@
         return (first, swap(first, "col", 1)), rest
 
     away_block = swap(block, "col", 2)
-    chip = [block, swap(block, "col", 1)]
-    away_chip = [away_block, swap(away_block, "col", 1)]
 
     def turned(pair):
         mine, other = pair[0].T, pair[1].T
@@ -417,10 +464,13 @@
         both = jnp.pad(both, ((0, 0), (0, lanes - depth)))
         return jnp.where(core == 0, both[:half], both[half:]), jnp.where(core == 0, both[half:], both[:half])
 
-    here, there = turned(chip), turned(away_chip)
+    def rest(*others):
+        away = after(away_block, *others)
+        return turned([away, swap(away, "col", 1)])
+
+    here = turned([block, swap(block, "col", 1)])
+    (_, there), terms, _ = through_columns(here, rest, turned_scalars)
     panel = [(jnp.where(x_at == 0, here[0], there[0]),), (jnp.where(x_at == 0, there[0], here[0]),)]
-
-    _, terms, _ = through_columns(here, lambda *_: there, turned_scalars)
     filter_one = sum(terms) / half_width
     panel_two, terms, _ = through_columns(*through_rows(filter_one, panel))
     filter_three = factor_two * sum(terms) - filter_one

time: 657 us -> 588 us (0.89)
  Pallas kernels: 359 us -> 289 us
  waiting for transfers between devices: 94 us -> 115 us
  local copies, waits for them, and re-layouts: 37.4 us -> 23.2 us
  other arithmetic: 29.7 us -> 20.8 us
    pallas_call x18, Pallas kernels: 199 us -> 161 us  [columns_product(): pl.pallas_call(kernel, out_shape=jax.ShapeDtypeStruct((count, vectors, wi...]
    pallas_call x12, Pallas kernels: 143 us -> 111 us  [rows_product(): pl.pallas_call(kernel, out_shape=jax.ShapeDtypeStruct((number, vectors, l...]
    ppermute x40, waiting for transfers between devices: 48.4 us -> 66.2 us  [around(): lax.ppermute(values, 'row', [(RING[p], RING[(p + way) % 8]) for p in rang...]
  transfers between devices with their start and end apart: 75 -> 75, of which waited for: 32 -> 46; matrix products, arithmetic and copies ran while one was open for 4% -> 4% of each run, Pallas kernels for 48% -> 46%
where the time goes in v2:
time: 588 us; the launch traced here: 579 us
  Pallas kernels  289 us (49%)
  starting transfers between devices  117 us (20%)
  waiting for transfers between devices  115 us (20%)
  local copies, waits for them, and re-layouts  23.2 us (4%)
  other arithmetic  20.8 us (4%)
  between operations  9.73 us (2%)
    pallas_call x18, Pallas kernels, columns_product(): pl.pallas_call(kernel, out_shape=jax.ShapeDtypeStruct((count, vectors, wi...  161 us
    pallas_call x12, Pallas kernels, rows_product(): pl.pallas_call(kernel, out_shape=jax.ShapeDtypeStruct((number, vectors, l...  111 us
    ppermute x33, starting transfers between devices, swap(): return lax.ppermute(values, axis, [(i, i ^ mask) for i in range(size)])  75.3 us
    ppermute x40, waiting for transfers between devices, around(): lax.ppermute(values, 'row', [(RING[p], RING[(p + way) % 8]) for p in rang...  66.2 us
    ppermute x33, waiting for transfers between devices, swap(): return lax.ppermute(values, axis, [(i, i ^ mask) for i in range(size)])  49 us
    ppermute x40, starting transfers between devices, around(): lax.ppermute(values, 'row', [(RING[p], RING[(p + way) % 8]) for p in rang...  34.1 us
    pallas_call x1, Pallas kernels, inverse_factor(): pl.pallas_call(kernel, out_shape=jax.ShapeDtypeStruct((size, size), F32),...  17.4 us
  transfers between devices with their start and end apart: 75, of which 46 were waited for; matrix products, arithmetic and copies ran while one was open for 4% of the time, Pallas kernels for 46%

profile of v2, /device:TPU:1, one launch (start us, length us, event | category | flops | bytes accessed | tf_op | source)
XLA Modules:
  0.0 578.7 jit_solution(9489277669638189764)
XLA Ops:
  36.4 7.4 %columns_product.22 = f32[2,256,768]{2,1,0:T(8,128)S(1)} custom-call(s32[3]{0:T(128)S(1)} %pad_add_fusion.2.scalars_ref, f32[1]{0:T(128)} %mul.68.center_ref, f32[2880,5760]{1,0:T(8,128)} %tile_ref.59, f32[128,1536]{1,0:T(8,128)S(1)} %get-tuple-element.84.refs_2_.refs_0_, f32[128,1536]{1,0:T(8,128)S(1)} %get-tuple-element.83.refs_3_.refs_1_, ...), custom_call_target="tpu_custom_call" | custom-call | flops 3397386240 | bytes 8847360 | tf_op jit(solution)/shard_map/columns_product/pallas_call | solution.py:190
  48.5 11.9 %columns_product.21 = f32[2,256,768]{2,1,0:T(8,128)S(1)} custom-call(s32[3]{0:T(128)S(1)} %pad_add_fusion.2.scalars_ref, f32[1]{0:T(128)} %mul.68.center_ref, f32[2880,5760]{1,0:T(8,128)} %tile_ref.59, f32[128,1536]{1,0:T(8,128)S(1)} %get-tuple-element.86.refs_0_, f32[128,1536]{1,0:T(8,128)S(1)} %get-tuple-element.85.refs_1_, ...), custom_call_target="tpu_custom_call" | custom-call | flops 6794772480 | bytes 17694720 | tf_op jit(solution)/shard_map/columns_product/pallas_call | solution.py:190
  66.3 16.4 %columns_product.20 = f32[3,256,768]{2,1,0:T(8,128)S(1)} custom-call(s32[3]{0:T(128)S(1)} %pad_add_fusion.2.scalars_ref, f32[1]{0:T(128)} %mul.68.center_ref, f32[2880,5760]{1,0:T(8,128)} %tile_ref.59, f32[128,1536]{1,0:T(8,128)S(1)} %get-tuple-element.86.refs_0_, f32[128,1536]{1,0:T(8,128)S(1)} %get-tuple-element.85.refs_1_, ...), custom_call_target="tpu_custom_call" | custom-call | flops 10192158720 | bytes 26542080 | tf_op jit(solution)/shard_map/columns_product/pallas_call | solution.py:190
  92.2 8.2 %collective-permute-done.6 = f32[256,768]{1,0:T(8,128)} collective-permute-done((f32[256,768]{1,0:T(8,128)S(1)}, f32[256,768]{1,0:T(8,128)}, u32[]{:S(2)}, u32[]{:S(2)}) %collective-permute-start.6) | collective-permute-done | bytes 786464 | tf_op jit(solution)/shard_map/ppermute | solution.py:357
  107.3 7.4 %rows_product.12.refs_2_ = f32[2,256,1536]{2,1,0:T(8,128)S(1)} custom-call(s32[3]{0:T(128)S(1)} %pad_add_fusion.scalars_ref, f32[1]{0:T(128)} %mul.68.center_ref, f32[2880,5760]{1,0:T(8,128)} %tile_ref.59, f32[256,768]{1,0:T(8,128)S(1)} %get-tuple-element.56.refs_0_), custom_call_target="tpu_custom_call" | custom-call | flops 3397386240 | bytes 8847360 | tf_op jit(solution)/shard_map/rows_product/pallas_call | solution.py:279
  122.1 12.3 %rows_product.13.refs_2_ = f32[2,256,1536]{2,1,0:T(8,128)S(1)} custom-call(s32[3]{0:T(128)S(1)} %pad_add_fusion.scalars_ref, f32[1]{0:T(128)} %mul.68.center_ref, f32[2880,5760]{1,0:T(8,128)} %tile_ref.59, f32[256,768]{1,0:T(8,128)S(1)} %collective-permute-done.11.refs_0_, f32[256,768]{1,0:T(8,128)S(1)} %collective-permute-done.13.refs_1_, ...), custom_call_target="tpu_custom_call" | custom-call | flops 6794772480 | bytes 17694720 | tf_op jit(solution)/shard_map/rows_product/pallas_call | solution.py:279
  138.5 12.4 %rows_product.14.refs_2_.refs_4_ = f32[2,256,1536]{2,1,0:T(8,128)S(1)} custom-call(s32[3]{0:T(128)S(1)} %pad_add_fusion.scalars_ref, f32[1]{0:T(128)} %mul.68.center_ref, f32[2880,5760]{1,0:T(8,128)} %tile_ref.59, f32[256,768]{1,0:T(8,128)S(1)} %collective-permute-done.12.refs_0_, f32[256,768]{1,0:T(8,128)S(1)} %collective-permute-done.15.refs_1_, ...), custom_call_target="tpu_custom_call" | custom-call | flops 6794772480 | bytes 17694720 | tf_op jit(solution)/shard_map/rows_product/pallas_call | solution.py:279
  154.3 7.7 %rows_product.15.refs_2_ = f32[1,256,1536]{2,1,0:T(8,128)S(1)} custom-call(s32[3]{0:T(128)S(1)} %pad_add_fusion.scalars_ref, f32[1]{0:T(128)} %mul.68.center_ref, f32[2880,5760]{1,0:T(8,128)} %tile_ref.59, f32[256,768]{1,0:T(8,128)S(1)} %collective-permute-done.14.refs_0_, f32[256,768]{1,0:T(8,128)S(1)} %collective-permute-done.17.refs_1_, ...), custom_call_target="tpu_custom_call" | custom-call | flops 3397386240 | bytes 8847360 | tf_op jit(solution)/shard_map/rows_product/pallas_call | solution.py:279
  168.0 9.1 %collective-permute-start.19 = (f32[128,1536]{1,0:T(8,128)S(1)}, f32[128,1536]{1,0:T(8,128)S(1)}, u32[]{:S(2)}, u32[]{:S(2)}) collective-permute-start(f32[128,1536]{1,0:T(8,128)S(1)} %slice_bitcast_fusion.16), channel_id=1, source_target_pairs={{0,1},{1,0},{2,3},{3,2},{4,5},{5,4},{6,7},{7,6},{8,9},{9,8},{10,11... | collective-permute-start | bytes 2359304 | tf_op jit(solution)/shard_map/ppermute | solution.py:353
  180.0 10.1 %rows_product.17 = f32[1,256,1536]{2,1,0:T(8,128)S(1)} custom-call(s32[3]{0:T(128)S(1)} %pad_add_fusion.scalars_ref, f32[1]{0:T(128)} %mul.68.center_ref, f32[2880,5760]{1,0:T(8,128)} %tile_ref.59, f32[256,768]{1,0:T(8,128)S(1)} %collective-permute-done.14.refs_0_, f32[256,768]{1,0:T(8,128)S(1)} %collective-permute-done.17.refs_1_, ...), custom_call_target="tpu_custom_call" | custom-call | flops 5096079360 | bytes 13271040 | tf_op jit(solution)/shard_map/rows_product/pallas_call | solution.py:279
  232.4 7.4 %columns_product.28 = f32[2,256,768]{2,1,0:T(8,128)S(1)} custom-call(s32[3]{0:T(128)S(1)} %pad_add_fusion.scalars_ref, f32[1]{0:T(128)} %mul.68.center_ref, f32[2880,5760]{1,0:T(8,128)} %tile_ref.59, f32[128,1536]{1,0:T(8,128)S(1)} %select_subtract_fusion.refs_2_.refs_0_, f32[128,1536]{1,0:T(8,128)S(1)} %collective-permute-done.24.refs_3_.refs_1_, ...), custom_call_target="tpu_custom_call" | custom-call | flops 3397386240 | bytes 8847360 | tf_op jit(solution)/shard_map/columns_product/pallas_call | solution.py:190
  243.2 11.9 %columns_product.27 = f32[2,256,768]{2,1,0:T(8,128)S(1)} custom-call(s32[3]{0:T(128)S(1)} %pad_add_fusion.scalars_ref, f32[1]{0:T(128)} %mul.68.center_ref, f32[2880,5760]{1,0:T(8,128)} %tile_ref.59, f32[128,1536]{1,0:T(8,128)S(1)} %select_subtract_fusion.1.refs_0_, f32[128,1536]{1,0:T(8,128)S(1)} %collective-permute-done.21.refs_1_, ...), custom_call_target="tpu_custom_call" | custom-call | flops 6794772480 | bytes 17694720 | tf_op jit(solution)/shard_map/columns_product/pallas_call | solution.py:190
  261.9 16.4 %columns_product.26 = f32[3,256,768]{2,1,0:T(8,128)S(1)} custom-call(s32[3]{0:T(128)S(1)} %pad_add_fusion.scalars_ref, f32[1]{0:T(128)} %mul.68.center_ref, f32[2880,5760]{1,0:T(8,128)} %tile_ref.59, f32[128,1536]{1,0:T(8,128)S(1)} %select_subtract_fusion.1.refs_0_, f32[128,1536]{1,0:T(8,128)S(1)} %collective-permute-done.21.refs_1_, ...), custom_call_target="tpu_custom_call" | custom-call | flops 10192158720 | bytes 26542080 | tf_op jit(solution)/shard_map/columns_product/pallas_call | solution.py:190
  280.1 14.1 %collective-permute-done.28 = f32[256,768]{1,0:T(8,128)S(1)} collective-permute-done((f32[256,768]{1,0:T(8,128)S(1)}, f32[256,768]{1,0:T(8,128)S(1)}, u32[]{:S(2)}, u32[]{:S(2)}) %collective-permute-start.28) | collective-permute-done | bytes 786464 | tf_op jit(solution)/shard_map/ppermute | solution.py:357
  314.2 12.3 %rows_product.19.refs_2_ = f32[2,256,1536]{2,1,0:T(8,128)S(1)} custom-call(s32[3]{0:T(128)S(1)} %pad_add_fusion.scalars_ref, f32[1]{0:T(128)} %mul.68.center_ref, f32[2880,5760]{1,0:T(8,128)} %tile_ref.59, f32[256,768]{1,0:T(8,128)S(1)} %collective-permute-done.33.refs_0_, f32[256,768]{1,0:T(8,128)S(1)} %collective-permute-done.35.refs_1_, ...), custom_call_target="tpu_custom_call" | custom-call | flops 6794772480 | bytes 17694720 | tf_op jit(solution)/shard_map/rows_product/pallas_call | solution.py:279
  330.2 12.4 %rows_product.20.refs_2_.refs_4_ = f32[2,256,1536]{2,1,0:T(8,128)S(1)} custom-call(s32[3]{0:T(128)S(1)} %pad_add_fusion.scalars_ref, f32[1]{0:T(128)} %mul.68.center_ref, f32[2880,5760]{1,0:T(8,128)} %tile_ref.59, f32[256,768]{1,0:T(8,128)S(1)} %collective-permute-done.34.refs_0_, f32[256,768]{1,0:T(8,128)S(1)} %collective-permute-done.37.refs_1_, ...), custom_call_target="tpu_custom_call" | custom-call | flops 6794772480 | bytes 17694720 | tf_op jit(solution)/shard_map/rows_product/pallas_call | solution.py:279
  346.8 7.7 %rows_product.21.refs_2_ = f32[1,256,1536]{2,1,0:T(8,128)S(1)} custom-call(s32[3]{0:T(128)S(1)} %pad_add_fusion.scalars_ref, f32[1]{0:T(128)} %mul.68.center_ref, f32[2880,5760]{1,0:T(8,128)} %tile_ref.59, f32[256,768]{1,0:T(8,128)S(1)} %collective-permute-done.36.refs_0_, f32[256,768]{1,0:T(8,128)S(1)} %collective-permute-done.39.refs_1_, ...), custom_call_target="tpu_custom_call" | custom-call | flops 3397386240 | bytes 8847360 | tf_op jit(solution)/shard_map/rows_product/pallas_call | solution.py:279
  360.0 7.9 %collective-permute-start.41 = (f32[128,1536]{1,0:T(8,128)S(1)}, f32[128,1536]{1,0:T(8,128)S(1)}, u32[]{:S(2)}, u32[]{:S(2)}) collective-permute-start(f32[128,1536]{1,0:T(8,128)S(1)} %slice_bitcast_fusion.7), channel_id=1, source_target_pairs={{0,1},{1,0},{2,3},{3,2},{4,5},{5,4},{6,7},{7,6},{8,9},{9,8},{10,11... | collective-permute-start | bytes 2359304 | tf_op jit(solution)/shard_map/ppermute | solution.py:353
  371.3 10.1 %rows_product.23 = f32[1,256,1536]{2,1,0:T(8,128)S(1)} custom-call(s32[3]{0:T(128)S(1)} %pad_add_fusion.scalars_ref, f32[1]{0:T(128)} %mul.68.center_ref, f32[2880,5760]{1,0:T(8,128)} %tile_ref.59, f32[256,768]{1,0:T(8,128)S(1)} %collective-permute-done.36.refs_0_, f32[256,768]{1,0:T(8,128)S(1)} %collective-permute-done.39.refs_1_, ...), custom_call_target="tpu_custom_call" | custom-call | flops 5096079360 | bytes 13271040 | tf_op jit(solution)/shard_map/rows_product/pallas_call | solution.py:279
  438.4 7.4 %columns_product.34 = f32[2,256,768]{2,1,0:T(8,128)S(1)} custom-call(s32[3]{0:T(128)S(1)} %pad_add_fusion.scalars_ref, f32[1]{0:T(128)} %mul.68.center_ref, f32[2880,5760]{1,0:T(8,128)} %tile_ref.59, f32[128,1536]{1,0:T(8,128)S(1)} %multiply_subtract_fusion.refs_2_.refs_0_, f32[128,1536]{1,0:T(8,128)S(1)} %collective-permute-done.46.refs_3_.refs_1_, ...), custom_call_target="tpu_custom_call" | custom-call | flops 3397386240 | bytes 8847360 | tf_op jit(solution)/shard_map/columns_product/pallas_call | solution.py:190
  455.7 11.9 %columns_product.33 = f32[2,256,768]{2,1,0:T(8,128)S(1)} custom-call(s32[3]{0:T(128)S(1)} %pad_add_fusion.scalars_ref, f32[1]{0:T(128)} %mul.68.center_ref, f32[2880,5760]{1,0:T(8,128)} %tile_ref.59, f32[128,1536]{1,0:T(8,128)S(1)} %multiply_subtract_fusion.1.refs_0_, f32[128,1536]{1,0:T(8,128)S(1)} %collective-permute-done.43.refs_1_, ...), custom_call_target="tpu_custom_call" | custom-call | flops 6794772480 | bytes 17694720 | tf_op jit(solution)/shard_map/columns_product/pallas_call | solution.py:190
  475.2 16.4 %columns_product.32 = f32[3,256,768]{2,1,0:T(8,128)S(1)} custom-call(s32[3]{0:T(128)S(1)} %pad_add_fusion.scalars_ref, f32[1]{0:T(128)} %mul.68.center_ref, f32[2880,5760]{1,0:T(8,128)} %tile_ref.59, f32[128,1536]{1,0:T(8,128)S(1)} %multiply_subtract_fusion.1.refs_0_, f32[128,1536]{1,0:T(8,128)S(1)} %collective-permute-done.43.refs_1_, ...), custom_call_target="tpu_custom_call" | custom-call | flops 10192158720 | bytes 26542080 | tf_op jit(solution)/shard_map/columns_product/pallas_call | solution.py:190
  510.8 17.4 %inverse_factor.1 = f32[256,256]{1,0:T(8,128)} custom-call(f32[256,256]{1,0:T(8,128)} %pad_maximum_fusion.8.gram_ref), custom_call_target="tpu_custom_call" | custom-call | flops 33554432 | bytes 524288 | tf_op jit(solution)/shard_map/inverse_factor/pallas_call | solution.py:340
  534.7 18.6 %collective-permute-start.67 = (f32[64,256]{1,0:T(8,128)S(1)}, f32[64,256]{1,0:T(8,128)S(1)}, u32[]{:S(2)}, u32[]{:S(2)}) collective-permute-start(f32[64,256]{1,0:T(8,128)S(1)} %slice_select_fusion.4), channel_id=1, source_target_pairs={{0,2},{1,3},{2,0},{3,1},{4,6},{5,7},{6,4},{7,5},{8,10},{9,11},{10,... | collective-permute-start | bytes 196616 | tf_op jit(solution)/shard_map/ppermute | solution.py:353
  (298 shorter events, 294.2 us)
Async XLA Ops:
  0.8 21.9 %collective-permute-start.1 = (f32[720,256]{1,0:T(8,128)}, f32[720,256]{1,0:T(8,128)}, u32[]{:S(2)}, u32[]{:S(2)}) collective-permute-start(f32[720,256]{1,0:T(8,128)} %param.8), channel_id=1, source_target_pairs={{0,2},{1,3},{2,0},{3,1},{4,6},{5,7},{6,4},{7,5},{8,10},{9,11},{10,... | collective-permute-start | bytes 2211848 | tf_op jit(solution)/shard_map/ppermute | solution.py:353
  46.6 17.6 %collective-permute-start.8 = (f32[256,768]{1,0:T(8,128)S(1)}, f32[256,768]{1,0:T(8,128)S(1)}, u32[]{:S(2)}, u32[]{:S(2)}) collective-permute-start(f32[256,768]{1,0:T(8,128)S(1)} %pad_maximum_fusion.3), channel_id=1, source_target_pairs={{0,4},{8,0},{16,8},{24,16},{28,24},{20,28},{12,20},{4,12},{1,5},{9... | collective-permute-start | bytes 2359304 | tf_op jit(solution)/shard_map/ppermute | solution.py:357
  46.9 17.7 %collective-permute-start.4 = (f32[256,768]{1,0:T(8,128)S(1)}, f32[256,768]{1,0:T(8,128)S(1)}, u32[]{:S(2)}, u32[]{:S(2)}) collective-permute-start(f32[256,768]{1,0:T(8,128)S(1)} %pad_maximum_fusion.2), channel_id=1, source_target_pairs={{0,8},{8,16},{16,24},{24,28},{28,20},{20,12},{12,4},{4,0},{1,9},{9... | collective-permute-start | bytes 2359304 | tf_op jit(solution)/shard_map/ppermute | solution.py:357
  64.8 18.0 %collective-permute-start.5 = (f32[256,768]{1,0:T(8,128)S(1)}, f32[256,768]{1,0:T(8,128)S(1)}, u32[]{:S(2)}, u32[]{:S(2)}) collective-permute-start(f32[256,768]{1,0:T(8,128)S(1)} %get-tuple-element.77), channel_id=1, source_target_pairs={{0,8},{8,16},{16,24},{24,28},{28,20},{20,12},{12,4},{4,0},{1,9},{9... | collective-permute-start | bytes 2359304 | tf_op jit(solution)/shard_map/ppermute | solution.py:357
  180.0 19.1 %collective-permute-start.20 = (f32[128,1536]{1,0:T(8,128)}, f32[128,1536]{1,0:T(8,128)}, u32[]{:S(2)}, u32[]{:S(2)}) collective-permute-start(f32[128,1536]{1,0:T(8,128)} %fusion.17), channel_id=1, source_target_pairs={{0,2},{1,3},{2,0},{3,1},{4,6},{5,7},{6,4},{7,5},{8,10},{9,11},{10,... | collective-permute-start | bytes 2359304 | tf_op jit(solution)/shard_map/ppermute | solution.py:353
  203.3 19.2 %collective-permute-start.23 = (f32[128,1536]{1,0:T(8,128)S(1)}, f32[128,1536]{1,0:T(8,128)S(1)}, u32[]{:S(2)}, u32[]{:S(2)}) collective-permute-start(f32[128,1536]{1,0:T(8,128)S(1)} %fusion.16), channel_id=1, source_target_pairs={{0,2},{1,3},{2,0},{3,1},{4,6},{5,7},{6,4},{7,5},{8,10},{9,11},{10,... | collective-permute-start | bytes 2359304 | tf_op jit(solution)/shard_map/ppermute | solution.py:353
  241.6 17.6 %collective-permute-start.30 = (f32[256,768]{1,0:T(8,128)S(1)}, f32[256,768]{1,0:T(8,128)S(1)}, u32[]{:S(2)}, u32[]{:S(2)}) collective-permute-start(f32[256,768]{1,0:T(8,128)S(1)} %pad_maximum_fusion.5), channel_id=1, source_target_pairs={{0,4},{8,0},{16,8},{24,16},{28,24},{20,28},{12,20},{4,12},{1,5},{9... | collective-permute-start | bytes 2359304 | tf_op jit(solution)/shard_map/ppermute | solution.py:357
  242.4 17.1 %collective-permute-start.26 = (f32[256,768]{1,0:T(8,128)S(1)}, f32[256,768]{1,0:T(8,128)S(1)}, u32[]{:S(2)}, u32[]{:S(2)}) collective-permute-start(f32[256,768]{1,0:T(8,128)S(1)} %pad_maximum_fusion.4), channel_id=1, source_target_pairs={{0,8},{8,16},{16,24},{24,28},{28,20},{20,12},{12,4},{4,0},{1,9},{9... | collective-permute-start | bytes 2359304 | tf_op jit(solution)/shard_map/ppermute | solution.py:357
  259.7 18.7 %collective-permute-start.27 = (f32[256,768]{1,0:T(8,128)S(1)}, f32[256,768]{1,0:T(8,128)S(1)}, u32[]{:S(2)}, u32[]{:S(2)}) collective-permute-start(f32[256,768]{1,0:T(8,128)S(1)} %get-tuple-element.71), channel_id=1, source_target_pairs={{0,8},{8,16},{16,24},{24,28},{28,20},{20,12},{12,4},{4,0},{1,9},{9... | collective-permute-start | bytes 2359304 | tf_op jit(solution)/shard_map/ppermute | solution.py:357
  260.9 17.5 %collective-permute-start.31 = (f32[256,768]{1,0:T(8,128)S(1)}, f32[256,768]{1,0:T(8,128)S(1)}, u32[]{:S(2)}, u32[]{:S(2)}) collective-permute-start(f32[256,768]{1,0:T(8,128)S(1)} %get-tuple-element.72), channel_id=1, source_target_pairs={{0,4},{8,0},{16,8},{24,16},{28,24},{20,28},{12,20},{4,12},{1,5},{9... | collective-permute-start | bytes 2359304 | tf_op jit(solution)/shard_map/ppermute | solution.py:357
  370.0 18.8 %collective-permute-start.42 = (f32[128,1536]{1,0:T(8,128)S(1)}, f32[128,1536]{1,0:T(8,128)S(1)}, u32[]{:S(2)}, u32[]{:S(2)}) collective-permute-start(f32[128,1536]{1,0:T(8,128)S(1)} %fusion.6), channel_id=1, source_target_pairs={{0,2},{1,3},{2,0},{3,1},{4,6},{5,7},{6,4},{7,5},{8,10},{9,11},{10,... | collective-permute-start | bytes 2359304 | tf_op jit(solution)/shard_map/ppermute | solution.py:353
  390.4 19.2 %collective-permute-start.45 = (f32[128,1536]{1,0:T(8,128)S(1)}, f32[128,1536]{1,0:T(8,128)S(1)}, u32[]{:S(2)}, u32[]{:S(2)}) collective-permute-start(f32[128,1536]{1,0:T(8,128)S(1)} %fusion.5), channel_id=1, source_target_pairs={{0,2},{1,3},{2,0},{3,1},{4,6},{5,7},{6,4},{7,5},{8,10},{9,11},{10,... | collective-permute-start | bytes 2359304 | tf_op jit(solution)/shard_map/ppermute | solution.py:353
  434.9 18.8 %collective-permute-start.62 = (f32[128,768]{1,0:T(8,128)S(1)}, f32[128,768]{1,0:T(8,128)S(1)}, u32[]{:S(2)}, u32[]{:S(2)}) collective-permute-start(f32[128,768]{1,0:T(8,128)S(1)} %get-tuple-element.89), channel_id=1, source_target_pairs={{0,4},{8,0},{16,8},{24,16},{28,24},{20,28},{12,20},{4,12},{1,5},{9... | collective-permute-start | bytes 1179656 | tf_op jit(solution)/shard_map/ppermute | solution.py:357
  435.0 18.7 %collective-permute-start.56 = (f32[128,768]{1,0:T(8,128)S(1)}, f32[128,768]{1,0:T(8,128)S(1)}, u32[]{:S(2)}, u32[]{:S(2)}) collective-permute-start(f32[128,768]{1,0:T(8,128)S(1)} %get-tuple-element.90), channel_id=1, source_target_pairs={{0,8},{8,16},{16,24},{24,28},{28,20},{20,12},{12,4},{4,0},{1,9},{9... | collective-permute-start | bytes 1179656 | tf_op jit(solution)/shard_map/ppermute | solution.py:357
  449.1 18.5 %collective-permute-start.55 = (f32[128,256]{1,0:T(8,128)S(1)}, f32[128,256]{1,0:T(8,128)S(1)}, u32[]{:S(2)}, u32[]{:S(2)}) collective-permute-start(f32[128,256]{1,0:T(8,128)S(1)} %pad_maximum_fusion.9), channel_id=1, source_target_pairs={{0,1},{1,0},{2,3},{3,2},{4,5},{5,4},{6,7},{7,6},{8,9},{9,8},{10,11... | collective-permute-start | bytes 393224 | tf_op jit(solution)/shard_map/ppermute | solution.py:353
  453.9 19.2 %collective-permute-start.57 = (f32[256,768]{1,0:T(8,128)S(1)}, f32[256,768]{1,0:T(8,128)S(1)}, u32[]{:S(2)}, u32[]{:S(2)}) collective-permute-start(f32[256,768]{1,0:T(8,128)S(1)} %pad_maximum_fusion.6), channel_id=1, source_target_pairs={{0,8},{8,16},{16,24},{24,28},{28,20},{20,12},{12,4},{4,0},{1,9},{9... | collective-permute-start | bytes 2359304 | tf_op jit(solution)/shard_map/ppermute | solution.py:357
  454.0 19.4 %collective-permute-start.63 = (f32[256,768]{1,0:T(8,128)S(1)}, f32[256,768]{1,0:T(8,128)S(1)}, u32[]{:S(2)}, u32[]{:S(2)}) collective-permute-start(f32[256,768]{1,0:T(8,128)S(1)} %pad_maximum_fusion.7), channel_id=1, source_target_pairs={{0,4},{8,0},{16,8},{24,16},{28,24},{20,28},{12,20},{4,12},{1,5},{9... | collective-permute-start | bytes 2359304 | tf_op jit(solution)/shard_map/ppermute | solution.py:357
  473.7 18.2 %collective-permute-start.64 = (f32[256,768]{1,0:T(8,128)S(1)}, f32[256,768]{1,0:T(8,128)S(1)}, u32[]{:S(2)}, u32[]{:S(2)}) collective-permute-start(f32[256,768]{1,0:T(8,128)S(1)} %get-tuple-element.65), channel_id=1, source_target_pairs={{0,4},{8,0},{16,8},{24,16},{28,24},{20,28},{12,20},{4,12},{1,5},{9... | collective-permute-start | bytes 2359304 | tf_op jit(solution)/shard_map/ppermute | solution.py:357
  474.8 17.6 %collective-permute-start.58 = (f32[256,768]{1,0:T(8,128)S(1)}, f32[256,768]{1,0:T(8,128)S(1)}, u32[]{:S(2)}, u32[]{:S(2)}) collective-permute-start(f32[256,768]{1,0:T(8,128)S(1)} %get-tuple-element.66), channel_id=1, source_target_pairs={{0,8},{8,16},{16,24},{24,28},{28,20},{20,12},{12,4},{4,0},{1,9},{9... | collective-permute-start | bytes 2359304 | tf_op jit(solution)/shard_map/ppermute | solution.py:357
  493.8 34.4 %collective-permute-start.65 = (f32[256,768]{1,0:T(8,128)}, f32[256,768]{1,0:T(8,128)}, u32[]{:S(2)}, u32[]{:S(2)}) collective-permute-start(f32[256,768]{1,0:T(8,128)} %get-tuple-element.58), channel_id=1, source_target_pairs={{0,4},{8,0},{16,8},{24,16},{28,24},{20,28},{12,20},{4,12},{1,5},{9... | collective-permute-start | bytes 2359304 | tf_op jit(solution)/shard_map/ppermute | solution.py:357
  494.6 33.6 %collective-permute-start.61 = (f32[256,768]{1,0:T(8,128)}, f32[256,768]{1,0:T(8,128)}, u32[]{:S(2)}, u32[]{:S(2)}) collective-permute-start(f32[256,768]{1,0:T(8,128)} %get-tuple-element.59), channel_id=1, source_target_pairs={{0,8},{8,16},{16,24},{24,28},{28,20},{20,12},{12,4},{4,0},{1,9},{9... | collective-permute-start | bytes 2359304 | tf_op jit(solution)/shard_map/ppermute | solution.py:357
  497.9 31.9 %collective-permute-start.60 = (f32[256,64]{1,0:T(8,128)}, f32[256,64]{1,0:T(8,128)}, u32[]{:S(2)}, u32[]{:S(2)}) collective-permute-start(f32[256,64]{1,0:T(8,128)} %slice.376), channel_id=1, source_target_pairs={{0,28},{8,29},{16,30},{24,31}} | collective-permute-start | bytes 196616 | tf_op jit(solution)/shard_map/ppermute | solution.py:518
  503.3 26.5 %collective-permute-start.59 = (f32[256,768]{1,0:T(8,128)S(1)}, f32[256,768]{1,0:T(8,128)S(1)}, u32[]{:S(2)}, u32[]{:S(2)}) collective-permute-start(f32[256,768]{1,0:T(8,128)S(1)} %constant_dynamic-slice_fusion), channel_id=1, source_target_pairs={{0,0},{1,8},{2,16},{3,24},{4,28},{5,20},{6,12},{7,4},{8,1},{9,9},{... | collective-permute-start | bytes 2359304 | tf_op jit(solution)/shard_map/ppermute | solution.py:516
  534.7 20.7 %collective-permute-start.67 = (f32[64,256]{1,0:T(8,128)S(1)}, f32[64,256]{1,0:T(8,128)S(1)}, u32[]{:S(2)}, u32[]{:S(2)}) collective-permute-start(f32[64,256]{1,0:T(8,128)S(1)} %slice_select_fusion.4), channel_id=1, source_target_pairs={{0,2},{1,3},{2,0},{3,1},{4,6},{5,7},{6,4},{7,5},{8,10},{9,11},{10,... | collective-permute-start | bytes 196616 | tf_op jit(solution)/shard_map/ppermute | solution.py:353
  (74 other events, 680.8 us)

commit v3 on v2

--- a/solution.py
+++ b/solution.py
@@ -14,6 +14,7 @@
 NN = (((1,), (0,)), ((), ()))
 BOTH = ("row", "col")
 RING = (0, 2, 4, 6, 7, 5, 3, 1)
+SPREAD = (0, 2, 1, 3)
 RING_AT = tuple(RING.index(r) for r in range(8))
 
 dot32 = functools.partial(lax.dot_general, preferred_element_type=F32)
@@ -330,9 +331,10 @@
             work[first : first + tall] = rows
             rest = first + tall
             if rest < size:
-                update = dot_exact(rows, rows, (((0,), (0,)), ((), ())))
+                skip = rest // LANES * LANES
+                update = dot_exact(rows[:, skip:], rows, (((0,), (0,)), ((), ())))
                 done = (lane >= first) & (lane < rest)
-                work[rest:] = jnp.where(done, 0.0, work[rest:]) - update[rest:]
+                work[rest:] = jnp.where(done, 0.0, work[rest:]) - update[rest - skip :]
         at_row = lax.broadcasted_iota(jnp.int32, (size, size), 0)
         at_lane = lax.broadcasted_iota(jnp.int32, (size, size), 1)
         out_ref[...] = jnp.where(at_lane <= at_row, work[...], 0.0)
@@ -406,8 +408,8 @@
     scalars, turned_scalars = (jnp.stack([place, offset, f]).astype(jnp.int32) for f in (jnp.int32(0), x_at))
 
     def through_columns(here, rest, scalars=scalars, before=None):
-        def product(call, aways, panel, **more):
-            told = scalars if before is None else after(scalars, *before(call))
+        def product(call, aways, panel, made=(), **more):
+            told = scalars if before is None else after(scalars, *before(call, *made))
             return columns_product(laplacian, told, centers, panel, aways, depth, width, **more)
 
         begun_far = product(0, (4,), [here])
@@ -416,7 +418,7 @@
         panel = [here, there]
         far = product(1, (4,), [there], first_chunk=1, totals=begun_far)[0]
         right, left = around(far[:half], 1), around(far[half:], -1)
-        ahead, behind = product(2, (3, -3), [there], first_chunk=1, totals=begun)
+        ahead, behind = product(2, (3, -3), [there], first_chunk=1, totals=begun, made=(far,))
         ahead = jnp.concatenate([ahead[:half] + right, ahead[half:]], 0)
         behind = jnp.concatenate([behind[:half], behind[half:] + left], 0)
         right, left = around(ahead, 1), around(behind, -1)
@@ -479,48 +481,42 @@
         mine, other = pieces
         return jnp.where(core == 0, jnp.concatenate([mine, other], 0), jnp.concatenate([other, mine], 0))
 
-    held = []
-
-    def whole_panel(here, there):
-        chunks = [straight(pair)[:, :depth] for pair in (here, there)]
-        chunk = jnp.where(x_at == 0, chunks[0], chunks[1])
-        own = jnp.where(core == 0, chunk[:, :own_rows], chunk[:, own_rows:])
-        held.append(sum_stages(dot_exact(own, own, NT)))
-        return chunks, own
-
-    def before(call):
-        for _ in range((0, 0, 1, 3, 3)[call]):
+    here, rest = through_rows(filter_three, panel_two)
+    held, got = [], []
+    lead = LANES
+    over = tile_rows - starts[4] * LANES
+
+    def rest_kept(*others):
+        got.append(rest(*others))
+        return got[0]
+
+    def before(call, *made):
+        if call == 2:
+            chunks = [straight(pair)[:, :depth] for pair in after((here, got[0]), *made)]
+            chunk = jnp.where(x_at == 0, chunks[0], chunks[1])
+            own = jnp.where(core == 0, chunk[:, :own_rows], chunk[:, own_rows:])
+            held.append(sum_stages(dot_exact(own, own, NT)))
+            padded = jnp.concatenate([jnp.zeros((vectors, lead), F32)] + chunks, 1)
+            part = row % per_tile
+            send_from = pick(starts, 4 * part + pick(SPREAD, col)) * LANES - part * tile_rows + lead
+            sent = lax.dynamic_slice_in_dim(padded, send_from, width, 1)
+            got.extend([own, sent, chunks[1][:, depth - over :]])
+        for _ in range((0, 0, 0, 2, 3)[call]):
             held.append(next(held[0]))
-        return held[-1:] if call > 1 else []
-
-    here, rest = through_rows(filter_three, panel_two)
-    got = []
-
-    def rest_and_gram(*others):
-        there = rest(*others)
-        got.append(whole_panel(here, there))
-        return there
-
-    _, (image, from_left, from_right), last_sent = through_columns(here, rest_and_gram, before=before)
-    panel_chunks, own = got[0]
+        return [] if call < 3 else held[-1:] + (got[2:] if call == 4 else [])
+
+    _, (image, from_left, from_right), last_sent = through_columns(here, rest_kept, before=before)
+    _, own, sent, sent_head = got
     filtered = own.T
-
-    lead = LANES
-    padded = jnp.concatenate([jnp.zeros((vectors, lead), F32)] + panel_chunks, 1)
-    part = row % per_tile
-    send_from = pick(starts, 4 * part + col) * LANES - part * tile_rows + lead
-    sent = lax.dynamic_slice_in_dim(padded, send_from, width, 1)
+    sent, sent_head = after((sent, sent_head), last_sent)
     pairs = [
-        (4 * r + c, 4 * RING[4 * (r % per_tile) + c] + r // per_tile) for r in range(8) for c in range(4)
+        (4 * r + c, 4 * RING[4 * (r % per_tile) + SPREAD[c]] + r // per_tile) for r in range(8) for c in range(4)
     ]
     moved = lax.ppermute(sent, BOTH, pairs)
-    over = tile_rows - starts[4] * LANES
-    head = lax.ppermute(
-        panel_chunks[1][:, depth - over :], BOTH, [(4 * (per_tile * c), 4 * RING[4] + c) for c in range(4)]
-    )
+    head = lax.ppermute(sent_head, BOTH, [(4 * (per_tile * c), 4 * RING[4] + c) for c in range(4)])
     moved = jnp.where(valid, moved + jnp.pad(head, ((0, 0), (0, width - over))), 0.0)
 
-    gram = held[-1]
+    *_, gram = held[0]
     inverse = inverse_factor(after(gram, last_sent))
     image = after(image, inverse) + from_left + from_right
     image = straight((image[:half], image[half:]))

time: 588 us -> 575 us (0.978)
  starting transfers between devices: 117 us -> 91.6 us
  waiting for transfers between devices: 115 us -> 124 us
    ppermute x33, starting transfers between devices: 75.3 us -> 52.9 us  [swap(): return lax.ppermute(values, axis, [(i, i ^ mask) for i in range(size)])]
    ppermute x1, waiting for transfers between devices: 0.01 us -> 14.7 us  [tuned_body(): moved = lax.ppermute(sent, BOTH, pairs)]
  transfers between devices with their start and end apart: 75 -> 75, of which waited for: 46 -> 41; matrix products, arithmetic and copies ran while one was open for 4% -> 5% of each run, Pallas kernels for 46% -> 47%
where the time goes in v3:
time: 575 us; the launch traced here: 565 us
  Pallas kernels  288 us (50%)
  waiting for transfers between devices  124 us (22%)
  starting transfers between devices  91.6 us (16%)
  local copies, waits for them, and re-layouts  25.5 us (4%)
  other arithmetic  21.3 us (4%)
  between operations  10 us (2%)
    pallas_call x18, Pallas kernels, columns_product(): pl.pallas_call(kernel, out_shape=jax.ShapeDtypeStruct((count, vectors, wi...  161 us
    pallas_call x12, Pallas kernels, rows_product(): pl.pallas_call(kernel, out_shape=jax.ShapeDtypeStruct((number, vectors, l...  111 us
    ppermute x40, waiting for transfers between devices, around(): lax.ppermute(values, 'row', [(RING[p], RING[(p + way) % 8]) for p in rang...  62.6 us
    ppermute x33, starting transfers between devices, swap(): return lax.ppermute(values, axis, [(i, i ^ mask) for i in range(size)])  52.9 us
    ppermute x33, waiting for transfers between devices, swap(): return lax.ppermute(values, axis, [(i, i ^ mask) for i in range(size)])  46.5 us
    ppermute x40, starting transfers between devices, around(): lax.ppermute(values, 'row', [(RING[p], RING[(p + way) % 8]) for p in rang...  34.5 us
    pallas_call x1, Pallas kernels, inverse_factor(): pl.pallas_call(kernel, out_shape=jax.ShapeDtypeStruct((size, size), F32),...  16.8 us
    ppermute x1, waiting for transfers between devices, tuned_body(): moved = lax.ppermute(sent, BOTH, pairs)  14.7 us
  transfers between devices with their start and end apart: 75, of which 41 were waited for; matrix products, arithmetic and copies ran while one was open for 5% of the time, Pallas kernels for 47%

profile of v3, /device:TPU:1, one launch (start us, length us, event | category | flops | bytes accessed | tf_op | source)
XLA Modules:
  0.0 564.6 jit_solution(14712784450119062492)
XLA Ops:
  36.3 7.4 %columns_product.22 = f32[2,256,768]{2,1,0:T(8,128)S(1)} custom-call(s32[3]{0:T(128)S(1)} %pad_add_fusion.2.scalars_ref, f32[1]{0:T(128)} %mul.71.center_ref, f32[2880,5760]{1,0:T(8,128)} %tile_ref.59, f32[128,1536]{1,0:T(8,128)S(1)} %get-tuple-element.94.refs_2_.refs_0_, f32[128,1536]{1,0:T(8,128)S(1)} %get-tuple-element.93.refs_3_.refs_1_, ...), custom_call_target="tpu_custom_call" | custom-call | flops 3397386240 | bytes 8847360 | tf_op jit(solution)/shard_map/columns_product/pallas_call | solution.py:191
  48.3 11.9 %columns_product.21 = f32[2,256,768]{2,1,0:T(8,128)S(1)} custom-call(s32[3]{0:T(128)S(1)} %pad_add_fusion.2.scalars_ref, f32[1]{0:T(128)} %mul.71.center_ref, f32[2880,5760]{1,0:T(8,128)} %tile_ref.59, f32[128,1536]{1,0:T(8,128)S(1)} %get-tuple-element.96.refs_0_, f32[128,1536]{1,0:T(8,128)S(1)} %get-tuple-element.95.refs_1_, ...), custom_call_target="tpu_custom_call" | custom-call | flops 6794772480 | bytes 17694720 | tf_op jit(solution)/shard_map/columns_product/pallas_call | solution.py:191
  66.2 16.4 %columns_product.20 = f32[3,256,768]{2,1,0:T(8,128)S(1)} custom-call(s32[3]{0:T(128)S(1)} %pad_add_fusion.2.scalars_ref, f32[1]{0:T(128)} %mul.71.center_ref, f32[2880,5760]{1,0:T(8,128)} %tile_ref.59, f32[128,1536]{1,0:T(8,128)S(1)} %get-tuple-element.96.refs_0_, f32[128,1536]{1,0:T(8,128)S(1)} %get-tuple-element.95.refs_1_, ...), custom_call_target="tpu_custom_call" | custom-call | flops 10192158720 | bytes 26542080 | tf_op jit(solution)/shard_map/columns_product/pallas_call | solution.py:191
  107.1 7.4 %rows_product.12.refs_2_ = f32[2,256,1536]{2,1,0:T(8,128)S(1)} custom-call(s32[3]{0:T(128)S(1)} %pad_add_fusion.scalars_ref, f32[1]{0:T(128)} %mul.71.center_ref, f32[2880,5760]{1,0:T(8,128)} %tile_ref.59, f32[256,768]{1,0:T(8,128)S(1)} %get-tuple-element.66.refs_0_), custom_call_target="tpu_custom_call" | custom-call | flops 3397386240 | bytes 8847360 | tf_op jit(solution)/shard_map/rows_product/pallas_call | solution.py:280
  122.0 12.3 %rows_product.13.refs_2_ = f32[2,256,1536]{2,1,0:T(8,128)S(1)} custom-call(s32[3]{0:T(128)S(1)} %pad_add_fusion.scalars_ref, f32[1]{0:T(128)} %mul.71.center_ref, f32[2880,5760]{1,0:T(8,128)} %tile_ref.59, f32[256,768]{1,0:T(8,128)S(1)} %collective-permute-done.11.refs_0_, f32[256,768]{1,0:T(8,128)S(1)} %collective-permute-done.13.refs_1_, ...), custom_call_target="tpu_custom_call" | custom-call | flops 6794772480 | bytes 17694720 | tf_op jit(solution)/shard_map/rows_product/pallas_call | solution.py:280
  138.3 12.4 %rows_product.14.refs_2_.refs_4_ = f32[2,256,1536]{2,1,0:T(8,128)S(1)} custom-call(s32[3]{0:T(128)S(1)} %pad_add_fusion.scalars_ref, f32[1]{0:T(128)} %mul.71.center_ref, f32[2880,5760]{1,0:T(8,128)} %tile_ref.59, f32[256,768]{1,0:T(8,128)S(1)} %collective-permute-done.12.refs_0_, f32[256,768]{1,0:T(8,128)S(1)} %collective-permute-done.15.refs_1_, ...), custom_call_target="tpu_custom_call" | custom-call | flops 6794772480 | bytes 17694720 | tf_op jit(solution)/shard_map/rows_product/pallas_call | solution.py:280
  154.1 7.7 %rows_product.15.refs_2_ = f32[1,256,1536]{2,1,0:T(8,128)S(1)} custom-call(s32[3]{0:T(128)S(1)} %pad_add_fusion.scalars_ref, f32[1]{0:T(128)} %mul.71.center_ref, f32[2880,5760]{1,0:T(8,128)} %tile_ref.59, f32[256,768]{1,0:T(8,128)S(1)} %collective-permute-done.14.refs_0_, f32[256,768]{1,0:T(8,128)S(1)} %collective-permute-done.17.refs_1_, ...), custom_call_target="tpu_custom_call" | custom-call | flops 3397386240 | bytes 8847360 | tf_op jit(solution)/shard_map/rows_product/pallas_call | solution.py:280
  167.9 9.1 %collective-permute-start.19 = (f32[128,1536]{1,0:T(8,128)S(1)}, f32[128,1536]{1,0:T(8,128)S(1)}, u32[]{:S(2)}, u32[]{:S(2)}) collective-permute-start(f32[128,1536]{1,0:T(8,128)S(1)} %slice_bitcast_fusion.16), channel_id=1, source_target_pairs={{0,1},{1,0},{2,3},{3,2},{4,5},{5,4},{6,7},{7,6},{8,9},{9,8},{10,11... | collective-permute-start | bytes 2359304 | tf_op jit(solution)/shard_map/ppermute | solution.py:355
  180.0 10.1 %rows_product.17 = f32[1,256,1536]{2,1,0:T(8,128)S(1)} custom-call(s32[3]{0:T(128)S(1)} %pad_add_fusion.scalars_ref, f32[1]{0:T(128)} %mul.71.center_ref, f32[2880,5760]{1,0:T(8,128)} %tile_ref.59, f32[256,768]{1,0:T(8,128)S(1)} %collective-permute-done.14.refs_0_, f32[256,768]{1,0:T(8,128)S(1)} %collective-permute-done.17.refs_1_, ...), custom_call_target="tpu_custom_call" | custom-call | flops 5096079360 | bytes 13271040 | tf_op jit(solution)/shard_map/rows_product/pallas_call | solution.py:280
  232.3 7.4 %columns_product.28 = f32[2,256,768]{2,1,0:T(8,128)S(1)} custom-call(s32[3]{0:T(128)S(1)} %pad_add_fusion.scalars_ref, f32[1]{0:T(128)} %mul.71.center_ref, f32[2880,5760]{1,0:T(8,128)} %tile_ref.59, f32[128,1536]{1,0:T(8,128)S(1)} %select_subtract_fusion.refs_2_.refs_0_, f32[128,1536]{1,0:T(8,128)S(1)} %collective-permute-done.24.refs_3_.refs_1_, ...), custom_call_target="tpu_custom_call" | custom-call | flops 3397386240 | bytes 8847360 | tf_op jit(solution)/shard_map/columns_product/pallas_call | solution.py:191
  243.1 11.9 %columns_product.27 = f32[2,256,768]{2,1,0:T(8,128)S(1)} custom-call(s32[3]{0:T(128)S(1)} %pad_add_fusion.scalars_ref, f32[1]{0:T(128)} %mul.71.center_ref, f32[2880,5760]{1,0:T(8,128)} %tile_ref.59, f32[128,1536]{1,0:T(8,128)S(1)} %select_subtract_fusion.1.refs_0_, f32[128,1536]{1,0:T(8,128)S(1)} %collective-permute-done.21.refs_1_, ...), custom_call_target="tpu_custom_call" | custom-call | flops 6794772480 | bytes 17694720 | tf_op jit(solution)/shard_map/columns_product/pallas_call | solution.py:191
  261.8 16.4 %columns_product.26 = f32[3,256,768]{2,1,0:T(8,128)S(1)} custom-call(s32[3]{0:T(128)S(1)} %pad_add_fusion.scalars_ref, f32[1]{0:T(128)} %mul.71.center_ref, f32[2880,5760]{1,0:T(8,128)} %tile_ref.59, f32[128,1536]{1,0:T(8,128)S(1)} %select_subtract_fusion.1.refs_0_, f32[128,1536]{1,0:T(8,128)S(1)} %collective-permute-done.21.refs_1_, ...), custom_call_target="tpu_custom_call" | custom-call | flops 10192158720 | bytes 26542080 | tf_op jit(solution)/shard_map/columns_product/pallas_call | solution.py:191
  280.0 14.0 %collective-permute-done.28 = f32[256,768]{1,0:T(8,128)S(1)} collective-permute-done((f32[256,768]{1,0:T(8,128)S(1)}, f32[256,768]{1,0:T(8,128)S(1)}, u32[]{:S(2)}, u32[]{:S(2)}) %collective-permute-start.28) | collective-permute-done | bytes 786464 | tf_op jit(solution)/shard_map/ppermute | solution.py:359
  297.7 7.4 %rows_product.18.refs_2_ = f32[2,256,1536]{2,1,0:T(8,128)S(1)} custom-call(s32[3]{0:T(128)S(1)} %pad_add_fusion.scalars_ref, f32[1]{0:T(128)} %mul.71.center_ref, f32[2880,5760]{1,0:T(8,128)} %tile_ref.59, f32[256,768]{1,0:T(8,128)S(1)} %fusion.15.refs_0_), custom_call_target="tpu_custom_call" | custom-call | flops 3397386240 | bytes 8847360 | tf_op jit(solution)/shard_map/rows_product/pallas_call | solution.py:280
  314.1 12.3 %rows_product.19.refs_2_ = f32[2,256,1536]{2,1,0:T(8,128)S(1)} custom-call(s32[3]{0:T(128)S(1)} %pad_add_fusion.scalars_ref, f32[1]{0:T(128)} %mul.71.center_ref, f32[2880,5760]{1,0:T(8,128)} %tile_ref.59, f32[256,768]{1,0:T(8,128)S(1)} %collective-permute-done.33.refs_0_, f32[256,768]{1,0:T(8,128)S(1)} %collective-permute-done.35.refs_1_, ...), custom_call_target="tpu_custom_call" | custom-call | flops 6794772480 | bytes 17694720 | tf_op jit(solution)/shard_map/rows_product/pallas_call | solution.py:280
  330.1 12.4 %rows_product.20.refs_2_.refs_4_ = f32[2,256,1536]{2,1,0:T(8,128)S(1)} custom-call(s32[3]{0:T(128)S(1)} %pad_add_fusion.scalars_ref, f32[1]{0:T(128)} %mul.71.center_ref, f32[2880,5760]{1,0:T(8,128)} %tile_ref.59, f32[256,768]{1,0:T(8,128)S(1)} %collective-permute-done.34.refs_0_, f32[256,768]{1,0:T(8,128)S(1)} %collective-permute-done.37.refs_1_, ...), custom_call_target="tpu_custom_call" | custom-call | flops 6794772480 | bytes 17694720 | tf_op jit(solution)/shard_map/rows_product/pallas_call | solution.py:280
  346.7 7.7 %rows_product.21.refs_2_ = f32[1,256,1536]{2,1,0:T(8,128)S(1)} custom-call(s32[3]{0:T(128)S(1)} %pad_add_fusion.scalars_ref, f32[1]{0:T(128)} %mul.71.center_ref, f32[2880,5760]{1,0:T(8,128)} %tile_ref.59, f32[256,768]{1,0:T(8,128)S(1)} %collective-permute-done.36.refs_0_, f32[256,768]{1,0:T(8,128)S(1)} %collective-permute-done.39.refs_1_, ...), custom_call_target="tpu_custom_call" | custom-call | flops 3397386240 | bytes 8847360 | tf_op jit(solution)/shard_map/rows_product/pallas_call | solution.py:280
  359.9 7.9 %collective-permute-start.41 = (f32[128,1536]{1,0:T(8,128)S(1)}, f32[128,1536]{1,0:T(8,128)S(1)}, u32[]{:S(2)}, u32[]{:S(2)}) collective-permute-start(f32[128,1536]{1,0:T(8,128)S(1)} %slice_bitcast_fusion.7), channel_id=1, source_target_pairs={{0,1},{1,0},{2,3},{3,2},{4,5},{5,4},{6,7},{7,6},{8,9},{9,8},{10,11... | collective-permute-start | bytes 2359304 | tf_op jit(solution)/shard_map/ppermute | solution.py:355
  371.2 10.1 %rows_product.23 = f32[1,256,1536]{2,1,0:T(8,128)S(1)} custom-call(s32[3]{0:T(128)S(1)} %pad_add_fusion.scalars_ref, f32[1]{0:T(128)} %mul.71.center_ref, f32[2880,5760]{1,0:T(8,128)} %tile_ref.59, f32[256,768]{1,0:T(8,128)S(1)} %collective-permute-done.36.refs_0_, f32[256,768]{1,0:T(8,128)S(1)} %collective-permute-done.39.refs_1_, ...), custom_call_target="tpu_custom_call" | custom-call | flops 5096079360 | bytes 13271040 | tf_op jit(solution)/shard_map/rows_product/pallas_call | solution.py:280
  425.9 7.4 %columns_product.34 = f32[2,256,768]{2,1,0:T(8,128)S(1)} custom-call(s32[3]{0:T(128)S(1)} %pad_add_fusion.scalars_ref, f32[1]{0:T(128)} %mul.71.center_ref, f32[2880,5760]{1,0:T(8,128)} %tile_ref.59, f32[128,1536]{1,0:T(8,128)S(1)} %multiply_subtract_fusion.refs_2_.refs_0_, f32[128,1536]{1,0:T(8,128)S(1)} %collective-permute-done.46.refs_3_.refs_1_, ...), custom_call_target="tpu_custom_call" | custom-call | flops 3397386240 | bytes 8847360 | tf_op jit(solution)/shard_map/columns_product/pallas_call | solution.py:191
  453.4 11.9 %columns_product.33 = f32[2,256,768]{2,1,0:T(8,128)S(1)} custom-call(s32[3]{0:T(128)S(1)} %pad_add_fusion.scalars_ref, f32[1]{0:T(128)} %mul.71.center_ref, f32[2880,5760]{1,0:T(8,128)} %tile_ref.59, f32[128,1536]{1,0:T(8,128)S(1)} %multiply_subtract_fusion.1.refs_0_, f32[128,1536]{1,0:T(8,128)S(1)} %collective-permute-done.43.refs_1_, ...), custom_call_target="tpu_custom_call" | custom-call | flops 6794772480 | bytes 17694720 | tf_op jit(solution)/shard_map/columns_product/pallas_call | solution.py:191
  470.9 16.4 %columns_product.32 = f32[3,256,768]{2,1,0:T(8,128)S(1)} custom-call(s32[3]{0:T(128)S(1)} %pad_add_fusion.scalars_ref, f32[1]{0:T(128)} %mul.71.center_ref, f32[2880,5760]{1,0:T(8,128)} %tile_ref.59, f32[128,1536]{1,0:T(8,128)S(1)} %multiply_subtract_fusion.1.refs_0_, f32[128,1536]{1,0:T(8,128)S(1)} %collective-permute-done.43.refs_1_, ...), custom_call_target="tpu_custom_call" | custom-call | flops 10192158720 | bytes 26542080 | tf_op jit(solution)/shard_map/columns_product/pallas_call | solution.py:191
  498.6 16.8 %inverse_factor.1 = f32[256,256]{1,0:T(8,128)} custom-call(f32[256,256]{1,0:T(8,128)} %pad_maximum_fusion.8.gram_ref), custom_call_target="tpu_custom_call" | custom-call | flops 33554432 | bytes 524288 | tf_op jit(solution)/shard_map/inverse_factor/pallas_call | solution.py:342
  517.9 14.7 %collective-permute-done.59 = f32[256,768]{1,0:T(8,128)} collective-permute-done((f32[256,768]{1,0:T(8,128)}, f32[256,768]{1,0:T(8,128)}, u32[]{:S(2)}, u32[]{:S(2)}) %collective-permute-start.59) | collective-permute-done | bytes 786464 | tf_op jit(solution)/shard_map/ppermute | solution.py:515
  (305 shorter events, 285.1 us)
Async XLA Ops:
  0.8 21.8 %collective-permute-start.1 = (f32[720,256]{1,0:T(8,128)}, f32[720,256]{1,0:T(8,128)}, u32[]{:S(2)}, u32[]{:S(2)}) collective-permute-start(f32[720,256]{1,0:T(8,128)} %param.9), channel_id=1, source_target_pairs={{0,2},{1,3},{2,0},{3,1},{4,6},{5,7},{6,4},{7,5},{8,10},{9,11},{10,... | collective-permute-start | bytes 2211848 | tf_op jit(solution)/shard_map/ppermute | solution.py:355
  46.5 17.6 %collective-permute-start.8 = (f32[256,768]{1,0:T(8,128)S(1)}, f32[256,768]{1,0:T(8,128)S(1)}, u32[]{:S(2)}, u32[]{:S(2)}) collective-permute-start(f32[256,768]{1,0:T(8,128)S(1)} %pad_maximum_fusion.3), channel_id=1, source_target_pairs={{0,4},{8,0},{16,8},{24,16},{28,24},{20,28},{12,20},{4,12},{1,5},{9... | collective-permute-start | bytes 2359304 | tf_op jit(solution)/shard_map/ppermute | solution.py:359
  46.7 17.7 %collective-permute-start.4 = (f32[256,768]{1,0:T(8,128)S(1)}, f32[256,768]{1,0:T(8,128)S(1)}, u32[]{:S(2)}, u32[]{:S(2)}) collective-permute-start(f32[256,768]{1,0:T(8,128)S(1)} %pad_maximum_fusion.2), channel_id=1, source_target_pairs={{0,8},{8,16},{16,24},{24,28},{28,20},{20,12},{12,4},{4,0},{1,9},{9... | collective-permute-start | bytes 2359304 | tf_op jit(solution)/shard_map/ppermute | solution.py:359
  64.6 18.0 %collective-permute-start.5 = (f32[256,768]{1,0:T(8,128)S(1)}, f32[256,768]{1,0:T(8,128)S(1)}, u32[]{:S(2)}, u32[]{:S(2)}) collective-permute-start(f32[256,768]{1,0:T(8,128)S(1)} %get-tuple-element.87), channel_id=1, source_target_pairs={{0,8},{8,16},{16,24},{24,28},{28,20},{20,12},{12,4},{4,0},{1,9},{9... | collective-permute-start | bytes 2359304 | tf_op jit(solution)/shard_map/ppermute | solution.py:359
  65.8 16.8 %collective-permute-start.9 = (f32[256,768]{1,0:T(8,128)S(1)}, f32[256,768]{1,0:T(8,128)S(1)}, u32[]{:S(2)}, u32[]{:S(2)}) collective-permute-start(f32[256,768]{1,0:T(8,128)S(1)} %get-tuple-element.88), channel_id=1, source_target_pairs={{0,4},{8,0},{16,8},{24,16},{28,24},{20,28},{12,20},{4,12},{1,5},{9... | collective-permute-start | bytes 2359304 | tf_op jit(solution)/shard_map/ppermute | solution.py:359
  179.9 19.1 %collective-permute-start.20 = (f32[128,1536]{1,0:T(8,128)}, f32[128,1536]{1,0:T(8,128)}, u32[]{:S(2)}, u32[]{:S(2)}) collective-permute-start(f32[128,1536]{1,0:T(8,128)} %fusion.17), channel_id=1, source_target_pairs={{0,2},{1,3},{2,0},{3,1},{4,6},{5,7},{6,4},{7,5},{8,10},{9,11},{10,... | collective-permute-start | bytes 2359304 | tf_op jit(solution)/shard_map/ppermute | solution.py:355
  203.2 19.2 %collective-permute-start.23 = (f32[128,1536]{1,0:T(8,128)S(1)}, f32[128,1536]{1,0:T(8,128)S(1)}, u32[]{:S(2)}, u32[]{:S(2)}) collective-permute-start(f32[128,1536]{1,0:T(8,128)S(1)} %fusion.16), channel_id=1, source_target_pairs={{0,2},{1,3},{2,0},{3,1},{4,6},{5,7},{6,4},{7,5},{8,10},{9,11},{10,... | collective-permute-start | bytes 2359304 | tf_op jit(solution)/shard_map/ppermute | solution.py:355
  241.4 17.6 %collective-permute-start.30 = (f32[256,768]{1,0:T(8,128)S(1)}, f32[256,768]{1,0:T(8,128)S(1)}, u32[]{:S(2)}, u32[]{:S(2)}) collective-permute-start(f32[256,768]{1,0:T(8,128)S(1)} %pad_maximum_fusion.5), channel_id=1, source_target_pairs={{0,4},{8,0},{16,8},{24,16},{28,24},{20,28},{12,20},{4,12},{1,5},{9... | collective-permute-start | bytes 2359304 | tf_op jit(solution)/shard_map/ppermute | solution.py:359
  242.4 17.1 %collective-permute-start.26 = (f32[256,768]{1,0:T(8,128)S(1)}, f32[256,768]{1,0:T(8,128)S(1)}, u32[]{:S(2)}, u32[]{:S(2)}) collective-permute-start(f32[256,768]{1,0:T(8,128)S(1)} %pad_maximum_fusion.4), channel_id=1, source_target_pairs={{0,8},{8,16},{16,24},{24,28},{28,20},{20,12},{12,4},{4,0},{1,9},{9... | collective-permute-start | bytes 2359304 | tf_op jit(solution)/shard_map/ppermute | solution.py:359
  259.7 18.6 %collective-permute-start.27 = (f32[256,768]{1,0:T(8,128)S(1)}, f32[256,768]{1,0:T(8,128)S(1)}, u32[]{:S(2)}, u32[]{:S(2)}) collective-permute-start(f32[256,768]{1,0:T(8,128)S(1)} %get-tuple-element.81), channel_id=1, source_target_pairs={{0,8},{8,16},{16,24},{24,28},{28,20},{20,12},{12,4},{4,0},{1,9},{9... | collective-permute-start | bytes 2359304 | tf_op jit(solution)/shard_map/ppermute | solution.py:359
  260.8 17.5 %collective-permute-start.31 = (f32[256,768]{1,0:T(8,128)S(1)}, f32[256,768]{1,0:T(8,128)S(1)}, u32[]{:S(2)}, u32[]{:S(2)}) collective-permute-start(f32[256,768]{1,0:T(8,128)S(1)} %get-tuple-element.82), channel_id=1, source_target_pairs={{0,4},{8,0},{16,8},{24,16},{28,24},{20,28},{12,20},{4,12},{1,5},{9... | collective-permute-start | bytes 2359304 | tf_op jit(solution)/shard_map/ppermute | solution.py:359
  311.6 17.0 %collective-permute-start.34 = (f32[256,768]{1,0:T(8,128)S(1)}, f32[256,768]{1,0:T(8,128)S(1)}, u32[]{:S(2)}, u32[]{:S(2)}) collective-permute-start(f32[256,768]{1,0:T(8,128)S(1)} %collective-permute-done.33.refs_0_), channel_id=1, source_target_pairs={{0,8},{8,16},{16,24},{24,28},{28,20},{20,12},{12,4},{4,0},{1,9},{9... | collective-permute-start | bytes 2359304 | tf_op jit(solution)/shard_map/ppermute | solution.py:359
  369.9 18.8 %collective-permute-start.42 = (f32[128,1536]{1,0:T(8,128)S(1)}, f32[128,1536]{1,0:T(8,128)S(1)}, u32[]{:S(2)}, u32[]{:S(2)}) collective-permute-start(f32[128,1536]{1,0:T(8,128)S(1)} %fusion.6), channel_id=1, source_target_pairs={{0,2},{1,3},{2,0},{3,1},{4,6},{5,7},{6,4},{7,5},{8,10},{9,11},{10,... | collective-permute-start | bytes 2359304 | tf_op jit(solution)/shard_map/ppermute | solution.py:355
  390.2 19.2 %collective-permute-start.45 = (f32[128,1536]{1,0:T(8,128)S(1)}, f32[128,1536]{1,0:T(8,128)S(1)}, u32[]{:S(2)}, u32[]{:S(2)}) collective-permute-start(f32[128,1536]{1,0:T(8,128)S(1)} %fusion.5), channel_id=1, source_target_pairs={{0,2},{1,3},{2,0},{3,1},{4,6},{5,7},{6,4},{7,5},{8,10},{9,11},{10,... | collective-permute-start | bytes 2359304 | tf_op jit(solution)/shard_map/ppermute | solution.py:355
  422.6 27.7 %collective-permute-start.62 = (f32[128,768]{1,0:T(8,128)}, f32[128,768]{1,0:T(8,128)}, u32[]{:S(2)}, u32[]{:S(2)}) collective-permute-start(f32[128,768]{1,0:T(8,128)} %get-tuple-element.99), channel_id=1, source_target_pairs={{0,4},{8,0},{16,8},{24,16},{28,24},{20,28},{12,20},{4,12},{1,5},{9... | collective-permute-start | bytes 1179656 | tf_op jit(solution)/shard_map/ppermute | solution.py:359
  424.5 25.8 %collective-permute-start.56 = (f32[128,768]{1,0:T(8,128)}, f32[128,768]{1,0:T(8,128)}, u32[]{:S(2)}, u32[]{:S(2)}) collective-permute-start(f32[128,768]{1,0:T(8,128)} %get-tuple-element.100), channel_id=1, source_target_pairs={{0,8},{8,16},{16,24},{24,28},{28,20},{20,12},{12,4},{4,0},{1,9},{9... | collective-permute-start | bytes 1179656 | tf_op jit(solution)/shard_map/ppermute | solution.py:359
  451.5 17.2 %collective-permute-start.57 = (f32[256,768]{1,0:T(8,128)S(1)}, f32[256,768]{1,0:T(8,128)S(1)}, u32[]{:S(2)}, u32[]{:S(2)}) collective-permute-start(f32[256,768]{1,0:T(8,128)S(1)} %pad_maximum_fusion.6), channel_id=1, source_target_pairs={{0,8},{8,16},{16,24},{24,28},{28,20},{20,12},{12,4},{4,0},{1,9},{9... | collective-permute-start | bytes 2359304 | tf_op jit(solution)/shard_map/ppermute | solution.py:359
  452.5 16.7 %collective-permute-start.63 = (f32[256,768]{1,0:T(8,128)S(1)}, f32[256,768]{1,0:T(8,128)S(1)}, u32[]{:S(2)}, u32[]{:S(2)}) collective-permute-start(f32[256,768]{1,0:T(8,128)S(1)} %pad_maximum_fusion.7), channel_id=1, source_target_pairs={{0,4},{8,0},{16,8},{24,16},{28,24},{20,28},{12,20},{4,12},{1,5},{9... | collective-permute-start | bytes 2359304 | tf_op jit(solution)/shard_map/ppermute | solution.py:359
  465.3 24.1 %collective-permute-start.54 = (f32[64,256]{1,0:T(8,128)S(1)}, f32[64,256]{1,0:T(8,128)S(1)}, u32[]{:S(2)}, u32[]{:S(2)}) collective-permute-start(f32[64,256]{1,0:T(8,128)S(1)} %pad_maximum_fusion.11), channel_id=1, source_target_pairs={{0,2},{1,3},{2,0},{3,1},{4,6},{5,7},{6,4},{7,5},{8,10},{9,11},{10,... | collective-permute-start | bytes 196616 | tf_op jit(solution)/shard_map/ppermute | solution.py:355
  469.3 17.9 %collective-permute-start.64 = (f32[256,768]{1,0:T(8,128)S(1)}, f32[256,768]{1,0:T(8,128)S(1)}, u32[]{:S(2)}, u32[]{:S(2)}) collective-permute-start(f32[256,768]{1,0:T(8,128)S(1)} %get-tuple-element.74), channel_id=1, source_target_pairs={{0,4},{8,0},{16,8},{24,16},{28,24},{20,28},{12,20},{4,12},{1,5},{9... | collective-permute-start | bytes 2359304 | tf_op jit(solution)/shard_map/ppermute | solution.py:359
  469.8 17.5 %collective-permute-start.58 = (f32[256,768]{1,0:T(8,128)S(1)}, f32[256,768]{1,0:T(8,128)S(1)}, u32[]{:S(2)}, u32[]{:S(2)}) collective-permute-start(f32[256,768]{1,0:T(8,128)S(1)} %get-tuple-element.75), channel_id=1, source_target_pairs={{0,8},{8,16},{16,24},{24,28},{28,20},{20,12},{12,4},{4,0},{1,9},{9... | collective-permute-start | bytes 2359304 | tf_op jit(solution)/shard_map/ppermute | solution.py:359
  487.5 28.7 %collective-permute-start.65 = (f32[256,768]{1,0:T(8,128)S(1)}, f32[256,768]{1,0:T(8,128)}, u32[]{:S(2)}, u32[]{:S(2)}) collective-permute-start(f32[256,768]{1,0:T(8,128)S(1)} %get-tuple-element.68), channel_id=1, source_target_pairs={{0,4},{8,0},{16,8},{24,16},{28,24},{20,28},{12,20},{4,12},{1,5},{9... | collective-permute-start | bytes 2359304 | tf_op jit(solution)/shard_map/ppermute | solution.py:359
  487.7 28.5 %collective-permute-start.61 = (f32[256,768]{1,0:T(8,128)S(1)}, f32[256,768]{1,0:T(8,128)}, u32[]{:S(2)}, u32[]{:S(2)}) collective-permute-start(f32[256,768]{1,0:T(8,128)S(1)} %get-tuple-element.69), channel_id=1, source_target_pairs={{0,8},{8,16},{16,24},{24,28},{28,20},{20,12},{12,4},{4,0},{1,9},{9... | collective-permute-start | bytes 2359304 | tf_op jit(solution)/shard_map/ppermute | solution.py:359
  494.5 38.1 %collective-permute-start.59 = (f32[256,768]{1,0:T(8,128)}, f32[256,768]{1,0:T(8,128)}, u32[]{:S(2)}, u32[]{:S(2)}) collective-permute-start(f32[256,768]{1,0:T(8,128)} %constant_dynamic-slice_fusion), channel_id=1, source_target_pairs={{0,0},{1,16},{2,8},{3,24},{4,28},{5,12},{6,20},{7,4},{8,1},{9,17},... | collective-permute-start | bytes 2359304 | tf_op jit(solution)/shard_map/ppermute | solution.py:515
  (77 other events, 704.5 us)
